TPU v7x, 256 devices: a whole 4x4x8 slice. The times are simulated.
256 devices in a mesh: dp: 4 (over x_lo, core), wide: 16 (over x_hi, z), narrow: 4 (over y).
Axes of the slice: x: 4 (x_hi: 2, x_lo: 2; x = x_hi * 2 + x_lo), y: 4, z: 8, core: 2. Of those that a mesh axis runs over, the one named last changes fastest.
Arguments:
- tokens: bfloat16 [8192, 4096], P(('wide', 'narrow')), may hold values from -6 to 6
- grads_out: bfloat16 [8192, 4096], P(('wide', 'narrow')), may hold values from -1.5 to 1.5
- expert_ids: int32 [8192, 2], P(('wide', 'narrow')), may hold values from 0 to 63, all different within a row; in each aligned block of 128 rows (0 to 127, 128 to 255, ...) at most 8 rows name the same one
- gates: float32 [8192, 2], P(('wide', 'narrow')), may hold values from 0.1 to 1
- w_gate: bfloat16 [64, 768, 4096], P(('wide', 'narrow'), 'dp'), may hold values from -0.09375 to 0.09375
- w_up: bfloat16 [64, 768, 4096], P(('wide', 'narrow'), 'dp'), may hold values from -0.09375 to 0.09375
- w_down: bfloat16 [64, 768, 4096], P(('wide', 'narrow'), 'dp'), may hold values from -0.21875 to 0.21875
Outputs:
- input_grad: bfloat16 [8192, 4096], P(('wide', 'narrow'), 'dp')
- gate_grad: float32 [8192, 2], P(('wide', 'narrow'))
- grad_gate: bfloat16 [64, 768, 4096], P(('wide', 'narrow'), 'dp')
- grad_up: bfloat16 [64, 768, 4096], P(('wide', 'narrow'), 'dp')
- grad_down: bfloat16 [64, 768, 4096], P(('wide', 'narrow'), 'dp')
Inputs may be any that keep to these rules, and one draw needn't show every extreme that they name: `expert_ids`: each token names 2 different experts. Among the 128 tokens of one group no expert is named by more than 8 tokens, a bound that some of them reach.
All inputs are finite; a program needn't handle non-finite values.
Results may differ from a plain program's by a relative error of at most 0.0075.
Values may be sent and summed in bfloat16 or wider, within the bound.
No kernel may reach another device: no remote copies, remote signals or barrier semaphores. Data moves between devices by JAX's collectives and lax.ppermute only.
A program may use at most 128 MiB of HBM per device.

v0:
```python
import jax
import jax.numpy as jnp
from jax import lax
from jax.sharding import PartitionSpec as P

TOP = 2


def silu_grad(values):
    sig = jax.nn.sigmoid(values)
    return sig * (1.0 + values * (1.0 - sig))


def body(tokens, grads_out, expert_ids, gates, w_gate, w_up, w_down):
    tok_rows, feature_width = tokens.shape
    wide_count = lax.axis_size("wide")
    narrow_count = lax.axis_size("narrow")
    experts = wide_count * narrow_count
    capacity = 2 * tok_rows * TOP // experts
    slot_count = experts * capacity
    flat_ids = expert_ids.reshape(-1)
    onehot = (flat_ids[:, None] == jnp.arange(experts, dtype=jnp.int32)[None, :]).astype(jnp.int32)
    earlier = jnp.cumsum(onehot, axis=0) - onehot
    position = flat_ids * capacity + jnp.sum(earlier * onehot, axis=1)
    chosen = (position[:, None] == jnp.arange(slot_count, dtype=jnp.int32)[None, :]).astype(
        jnp.float32
    )
    chosen = chosen.reshape(tok_rows, TOP, slot_count)
    placing = jnp.sum(chosen, axis=1).astype(jnp.bfloat16)
    sent_tokens = jnp.einsum(
        "ts,td->sd", placing, tokens, preferred_element_type=jnp.float32
    ).astype(jnp.bfloat16)
    sent_grads = jnp.einsum(
        "ts,td->sd", placing, grads_out, preferred_element_type=jnp.float32
    ).astype(jnp.bfloat16)
    shaped = (experts, capacity, feature_width)
    got_tokens, got_grads = (
        lax.all_to_all(
            sent_tokens.reshape(shaped), ("wide", "narrow"), split_axis=0, concat_axis=0, tiled=True
        ),
        lax.all_to_all(
            sent_grads.reshape(shaped), ("wide", "narrow"), split_axis=0, concat_axis=0, tiled=True
        ),
    )
    token_rows = got_tokens.reshape(slot_count, feature_width)
    grad_rows = got_grads.reshape(slot_count, feature_width)
    gate_mat = w_gate[0]
    up_mat = w_up[0]
    down_mat = w_down[0]
    gate_pre = jnp.einsum("rd,hd->rh", token_rows, gate_mat, preferred_element_type=jnp.float32)
    up_pre = jnp.einsum("rd,hd->rh", token_rows, up_mat, preferred_element_type=jnp.float32)
    activated = jax.nn.silu(gate_pre)
    hidden = (activated * up_pre).astype(jnp.bfloat16)
    hidden_grad = jnp.einsum("rd,hd->rh", grad_rows, down_mat, preferred_element_type=jnp.float32)
    gate_dot = jnp.sum(hidden.astype(jnp.float32) * hidden_grad, axis=1)
    up_grad = (hidden_grad * activated).astype(jnp.bfloat16)
    pre_grad = (hidden_grad * up_pre * silu_grad(gate_pre)).astype(jnp.bfloat16)
    grad_down = jnp.einsum(
        "rh,rd->hd", hidden, grad_rows, preferred_element_type=jnp.float32
    ).astype(jnp.bfloat16)
    grad_gate = jnp.einsum(
        "rh,rd->hd", pre_grad, token_rows, preferred_element_type=jnp.float32
    ).astype(jnp.bfloat16)
    grad_up = jnp.einsum(
        "rh,rd->hd", up_grad, token_rows, preferred_element_type=jnp.float32
    ).astype(jnp.bfloat16)
    row_grad = jnp.einsum("rh,hd->rd", pre_grad, gate_mat, preferred_element_type=jnp.float32)
    row_grad = row_grad + jnp.einsum(
        "rh,hd->rd", up_grad, up_mat, preferred_element_type=jnp.float32
    )
    part_width = row_grad.shape[1]
    back_grad, back_dot = (
        lax.all_to_all(
            row_grad.reshape(experts, capacity, part_width),
            ("wide", "narrow"),
            split_axis=0,
            concat_axis=0,
            tiled=True,
        ),
        lax.all_to_all(
            gate_dot.reshape(experts, capacity),
            ("wide", "narrow"),
            split_axis=0,
            concat_axis=0,
            tiled=True,
        ),
    )
    back_grad = back_grad.reshape(slot_count, part_width)
    back_dot = back_dot.reshape(slot_count)
    pair_rows = jnp.take(back_grad, position, axis=0).reshape(tok_rows, TOP, part_width)
    token_grad = jnp.sum(pair_rows * gates[:, :, None], axis=1)
    token_dots = jnp.take(back_dot, position).reshape(tok_rows, TOP)
    input_grad = lax.psum_scatter(token_grad, "dp", scatter_dimension=1, tiled=True)
    gate_grad = lax.psum(token_dots, "dp")
    return (
        input_grad.astype(jnp.bfloat16),
        gate_grad,
        grad_gate[None],
        grad_up[None],
        grad_down[None],
    )


def solution(mesh):
    in_specs = (
        P(("wide", "narrow"), None),
        P(("wide", "narrow"), None),
        P(("wide", "narrow"), None),
        P(("wide", "narrow"), None),
        P(("wide", "narrow"), "dp", None),
        P(("wide", "narrow"), "dp", None),
        P(("wide", "narrow"), "dp", None),
    )
    out_specs = (
        P(("wide", "narrow"), "dp"),
        P(("wide", "narrow"), None),
        P(("wide", "narrow"), "dp", None),
        P(("wide", "narrow"), "dp", None),
        P(("wide", "narrow"), "dp", None),
    )
    return jax.shard_map(body, mesh=mesh, in_specs=in_specs, out_specs=out_specs, check_vma=False)
```

profile of v0, /device:TPU:24, one launch (start us, length us, event | category | flops | bytes accessed | tf_op | source)
XLA Modules:
  0.0 509.1 jit_solution(14192318668211924256)
XLA Ops:
  7.2 0.0 copy-start
  7.2 0.9 copy.28
  8.1 0.1 eq.40
  8.2 0.1 reshape.116
  8.4 0.6 reduce-window.6
  9.0 0.2 slice_reduce_fusion
  9.2 0.1 fusion.23
  9.3 0.1 reduce_sum.41
  9.5 0.6 broadcast_multiply_fusion
  10.1 0.6 copy-done.4
  10.8 0.1 copy.32
  10.8 0.1 convert_reduce_fusion
  11.0 4.4 fusion.1
  15.4 14.7 %all-to-all-start.1 = ((bf16[64,8,4096]{2,1,0:T(8,128)(2,1)}), bf16[64,8,4096]{2,1,0:T(8,128)(2,1)}, u32[]{:S(2)}, u32[]{:S(2)}) async-start(bf16[64,8,4096]{2,1,0:T(8,128)(2,1)} %fusion.1), calls=%async_computation.1 | async-start | bytes 8388608 | tf_op jit(solution)/shard_map/all_to_all | solution.py:38
  30.1 3.2 fusion
  33.3 93.8 %all-to-all-done.1 = bf16[64,8,4096]{2,1,0:T(8,128)(2,1)} async-done(((bf16[64,8,4096]{2,1,0:T(8,128)(2,1)}), bf16[64,8,4096]{2,1,0:T(8,128)(2,1)}, u32[]{:S(2)}, u32[]{:S(2)}) %all-to-all-start.1) | async-done | bytes 4194336 | tf_op jit(solution)/shard_map/all_to_all | solution.py:38
  127.1 6.3 %all-to-all-start = ((bf16[64,8,4096]{2,1,0:T(8,128)(2,1)}), bf16[64,8,4096]{2,1,0:T(8,128)(2,1)}, u32[]{:S(2)}, u32[]{:S(2)}) async-start(bf16[64,8,4096]{2,1,0:T(8,128)(2,1)} %fusion), calls=%async_computation | async-start | bytes 8388608 | tf_op jit(solution)/shard_map/all_to_all | solution.py:41
  133.4 0.0 copy-start.2
  133.4 4.6 fusion.7
  138.0 4.5 fusion.9
  142.5 87.9 %all-to-all-done = bf16[64,8,4096]{2,1,0:T(8,128)(2,1)} async-done(((bf16[64,8,4096]{2,1,0:T(8,128)(2,1)}), bf16[64,8,4096]{2,1,0:T(8,128)(2,1)}, u32[]{:S(2)}, u32[]{:S(2)}) %all-to-all-start) | async-done | bytes 4194336 | tf_op jit(solution)/shard_map/all_to_all | solution.py:41
  230.4 5.1 %multiply_reduce_fusion.1 = (f32[512]{0:T(512)S(1)}, bf16[512,192]{0,1:T(8,128)(2,1)}, bf16[512,192]{0,1:T(8,128)(2,1)S(1)}, bf16[512,192]{0,1:T(8,128)(2,1)S(1)}) fusion(f32[512,192]{0,1:T(8,128)} %fusion.9, f32[512,192]{0,1:T(8,128)} %fusion.7, bf16[1,192,4096]{2,1,0:T(8,128)(2,1)} %param.13, bf16[64,8,4096]{2,1,0:T(8,128)(2,1)} %all-to-all-done), kind=kOutput, calls=%fused_computation.31 | convolution fusion | flops 807075328 | bytes 7145472 | tf_op jit(solution)/shard_map/rd,hd->rh/dot_general | solution.py:54
  235.5 0.7 all_to_all.18
  236.2 6.2 %all-to-all-start.3 = ((f32[64,1,8]{2,1,0:T(1,128)}), f32[64,1,8]{2,1,0:T(1,128)}, u32[]{:S(2)}, u32[]{:S(2)}) async-start(f32[64,1,8]{2,1,0:T(1,128)} %bitcast.75), calls=%async_computation.4 | async-start | bytes 65536 | tf_op jit(solution)/shard_map/all_to_all | solution.py:80
  242.4 1.3 fusion.14
  243.7 4.5 add_bitcast_fusion
  248.2 4.7 all-to-all-done.3
  253.0 8.4 %all-to-all-start.2 = ((f32[64,8,4096]{2,1,0:T(8,128)}), f32[64,8,4096]{2,1,0:T(8,128)}, u32[]{:S(2)}, u32[]{:S(2)}) async-start(f32[64,8,4096]{2,1,0:T(8,128)} %add_bitcast_fusion), calls=%async_computation.2 | async-start | bytes 16777216 | tf_op jit(solution)/shard_map/all_to_all | solution.py:73
  261.4 0.0 reduce-scatter.2.cloned.1.call-start
  261.4 0.1 mul.68
  261.6 0.1 copy.33
  261.7 0.5 broadcast.98
  262.2 1.5 reduce.5
  263.7 0.1 reshape.124
  263.8 1.9 gather_fusion.1
  265.8 0.1 gather.15
  266.0 181.0 %all-to-all-done.2 = f32[64,8,4096]{2,1,0:T(8,128)} async-done(((f32[64,8,4096]{2,1,0:T(8,128)}), f32[64,8,4096]{2,1,0:T(8,128)}, u32[]{:S(2)}, u32[]{:S(2)}) %all-to-all-start.2) | async-done | bytes 8388640 | tf_op jit(solution)/shard_map/all_to_all | solution.py:73
  446.9 9.0 %gather_fusion = f32[256,4096]{1,0:T(8,128)} fusion(f32[512,4096]{1,0:T(8,128)} %bitcast.9, s32[1024]{0:T(1024)S(1)} %pad_clamp_fusion), kind=kCustom, calls=%fused_computation | custom fusion | bytes 8389632 | tf_op jit(solution)/shard_map/jit(_take)/gather | solution.py:90
  456.0 5.8 %gather.13 = f32[128,2,4096]{2,1,0:T(2,128)} reshape(f32[256,4096]{1,0:T(8,128)} %gather_fusion) | data formatting | bytes 8388608 | tf_op jit(solution)/shard_map/jit(_take)/gather | solution.py:90
  461.8 11.2 %multiply_reduce_fusion = f32[128,4096]{1,0:T(8,128)} fusion(f32[128,2,4096]{2,1,0:T(2,128)} %gather.13, pred[128,2]{1,0:T(8,128)(4,1)S(1)} %get-tuple-element.21, f32[128,2]{1,0:T(8,128)S(1)} %copy.33), kind=kLoop, calls=%fused_computation.22 | loop fusion | flops 2621440 | bytes 6292736 | tf_op jit(solution)/shard_map/reduce_sum | solution.py:91
  473.0 0.0 reduce-scatter.2.cloned.1.call-update
  473.1 4.3 fusion.2
  477.4 4.5 fusion.3
  481.8 4.3 fusion.4
  486.2 13.4 %psum.7 = f32[128,2]{1,0:T(8,128)S(1)} all-reduce(f32[128,2]{1,0:T(8,128)S(1)} %get-tuple-element.20), channel_id=1, replica_groups=mesh['dp'=4,'wide'=16,'narrow'=4] {'dp'}, use_global_device_ids=true, to_apply=%region_7.8 | all-reduce | flops 256 | bytes 2048 | tf_op jit(solution)/shard_map/psum | solution.py:94
  499.6 0.6 copy.35
  500.2 0.3 reduce-scatter.2.cloned.1.call-done
  500.5 1.8 convert_element_type.52
  (21 shorter events, 0.1 us)
Async XLA Ops:
  7.2 126.2 %copy-start = (bf16[1,192,4096]{2,1,0:T(8,128)(2,1)S(1)}, bf16[1,192,4096]{2,1,0:T(8,128)(2,1)}, u32[]{:S(2)}) copy-start(bf16[1,192,4096]{2,1,0:T(8,128)(2,1)} %param.11) | copy-start | bytes 4718596
  10.1 0.6 copy-start.4
  15.4 14.7 %copy-start.3 = (bf16[128,4096]{1,0:T(8,128)(2,1)S(1)}, bf16[128,4096]{1,0:T(8,128)(2,1)}, u32[]{:S(2)}) copy-start(bf16[128,4096]{1,0:T(8,128)(2,1)} %param.8) | copy-start | bytes 3145732
  15.4 111.7 %all-to-all-start.1 = ((bf16[64,8,4096]{2,1,0:T(8,128)(2,1)}), bf16[64,8,4096]{2,1,0:T(8,128)(2,1)}, u32[]{:S(2)}, u32[]{:S(2)}) async-start(bf16[64,8,4096]{2,1,0:T(8,128)(2,1)} %fusion.1), calls=%async_computation.1 | async-start | bytes 8388608 | tf_op jit(solution)/shard_map/all_to_all | solution.py:38
  127.1 103.3 %all-to-all-start = ((bf16[64,8,4096]{2,1,0:T(8,128)(2,1)}), bf16[64,8,4096]{2,1,0:T(8,128)(2,1)}, u32[]{:S(2)}, u32[]{:S(2)}) async-start(bf16[64,8,4096]{2,1,0:T(8,128)(2,1)} %fusion), calls=%async_computation | async-start | bytes 8388608 | tf_op jit(solution)/shard_map/all_to_all | solution.py:41
  133.4 4.6 copy-start.2
  236.2 16.8 %all-to-all-start.3 = ((f32[64,1,8]{2,1,0:T(1,128)}), f32[64,1,8]{2,1,0:T(1,128)}, u32[]{:S(2)}, u32[]{:S(2)}) async-start(f32[64,1,8]{2,1,0:T(1,128)} %bitcast.75), calls=%async_computation.4 | async-start | bytes 65536 | tf_op jit(solution)/shard_map/all_to_all | solution.py:80
  248.2 13.2 %copy-start.6 = (s32[128,2]{1,0:T(8,128)S(1)}, s32[128,2]{1,0:T(8,128)}, u32[]{:S(2)}) copy-start(s32[128,2]{1,0:T(8,128)} %get-tuple-element.26) | copy-start | bytes 3076
  248.2 13.3 %copy-start.8 = (f32[128,2]{0,1:T(2,128)S(1)}, f32[128,2]{0,1:T(2,128)}, u32[]{:S(2)}) copy-start(f32[128,2]{0,1:T(2,128)} %param.10) | copy-start | bytes 3076
  248.2 17.7 %copy-start.5 = (s32[128,2]{1,0:T(8,128)S(1)}, s32[128,2]{1,0:T(8,128)}, u32[]{:S(2)}) copy-start(s32[128,2]{1,0:T(8,128)} %copy-done.4) | copy-start | bytes 3076
  253.0 193.9 %all-to-all-start.2 = ((f32[64,8,4096]{2,1,0:T(8,128)}), f32[64,8,4096]{2,1,0:T(8,128)}, u32[]{:S(2)}, u32[]{:S(2)}) async-start(f32[64,8,4096]{2,1,0:T(8,128)} %add_bitcast_fusion), calls=%async_computation.2 | async-start | bytes 16777216 | tf_op jit(solution)/shard_map/all_to_all | solution.py:73
  261.4 239.1 %reduce-scatter.2.cloned.1.call-start = ((), (), s32[]{:S(2)}) async-start(), calls=%async_computation.5 | async-start | bytes 2621440 | tf_op jit(solution)/shard_map/reduce_scatter | solution.py:93
  477.4 4.5 copy-start.7
  477.4 24.9 %copy-start.1 = (bf16[1,192,4096]{2,1,0:T(8,128)(2,1)S(1)}, bf16[1,192,4096]{2,1,0:T(8,128)(2,1)}, u32[]{:S(2)}) copy-start(bf16[1,192,4096]{2,1,0:T(8,128)(2,1)} %param.11) | copy-start | bytes 4718596
Sparse Core Ops, SparseCore 0:
  473.2 27.2 reduce-scatter.1
where the time goes:
time: 511 us; the launch traced here: 509 us
  waiting for transfers between devices  368 us (72%)
  matrix products  40.8 us (8%)
  starting transfers between devices  35.6 us (7%)
  local copies, waits for them, and re-layouts  21.4 us (4%)
  other arithmetic  16.1 us (3%)
  between operations  14.2 us (3%)
  blocking collectives  13.4 us (3%)
    all_to_all x1, waiting for transfers between devices, body(): lax.all_to_all(row_grad.reshape(experts, capacity, part_width), ('wide',...  181 us
    all_to_all x1, waiting for transfers between devices, body(): lax.all_to_all(sent_tokens.reshape(shaped), ('wide', 'narrow'), split_axi...  93.8 us
    all_to_all x1, waiting for transfers between devices, body(): lax.all_to_all(sent_grads.reshape(shaped), ('wide', 'narrow'), split_axis...  87.9 us
    gather x2, local copies, waits for them, and re-layouts, body(): jnp.take(back_grad, position, axis=0).reshape(tok_rows, TOP, part_width)  14.9 us
    all_to_all x1, starting transfers between devices, body(): lax.all_to_all(sent_tokens.reshape(shaped), ('wide', 'narrow'), split_axi...  14.7 us
    psum x1, blocking collectives, body(): gate_grad = lax.psum(token_dots, 'dp')  13.4 us
    reduce_sum x1, other arithmetic, body(): token_grad = jnp.sum(pair_rows * gates[:, :, None], axis=1)  11.2 us
  transfers between devices with their start and end apart: 5, of which 5 were waited for; matrix products, arithmetic and copies ran while one was open for 7% of the time, Pallas kernels for 0%

commit v1 on v0

v1 whole, which is shorter than its diff:
```python
import functools

import jax
import jax.numpy as jnp
from jax import lax
from jax.experimental import pallas as pl
from jax.experimental.pallas import tpu as pltpu
from jax.sharding import Mesh, PartitionSpec as P

F32 = jnp.float32
BF16 = jnp.bfloat16
LANES = 128
VMEM_LIMIT = 56 * 1024 * 1024
ROWS = ("xhi", "z", "y")
PARTS = ("xlo", "core")


def silu_grad(values):
    sig = jax.nn.sigmoid(values)
    return sig * (1.0 + values * (1.0 - sig))


def dot(a, b, dims):
    return lax.dot_general(a, b, (dims, ((), ())), preferred_element_type=F32)


NN = ((1,), (0,))
NT = ((1,), (1,))
TN = ((0,), (0,))


def three_parts(value):
    high = value.astype(BF16)
    rest = value - high.astype(F32)
    middle = rest.astype(BF16)
    return high, middle, (rest - middle.astype(F32)).astype(BF16)


def in_lanes(parts, rows):
    lane = lax.broadcasted_iota(jnp.int32, (rows, LANES), 1)
    block = jnp.zeros((rows, LANES), F32)
    for i, part in enumerate(parts):
        block = jnp.where(lane == i, part.astype(F32), block)
    return block.astype(BF16)


def call(kernel, outs, args, flops, smem=0):
    moved = sum(a.size * a.dtype.itemsize for a in args) + sum(
        int(jnp.dtype(t).itemsize) * functools.reduce(lambda x, y: x * y, s, 1) for s, t in outs
    )
    vmem = pl.BlockSpec(memory_space=pltpu.VMEM)
    result = pl.pallas_call(
        kernel,
        out_shape=[jax.ShapeDtypeStruct(s, t) for s, t in outs],
        in_specs=[vmem] * len(args),
        out_specs=[vmem] * len(outs),
        compiler_params=pltpu.CompilerParams(vmem_limit_bytes=VMEM_LIMIT),
        cost_estimate=pl.CostEstimate(flops=flops, bytes_accessed=moved, transcendentals=0),
    )(*args)
    return result


def columns(start_block, width):
    return pl.ds(pl.multiple_of(start_block * width, LANES), width)


def place_tokens(capacity, ids_ref, tokens_ref, sent_ref, first_ref, second_ref):
    slots, quarter = sent_ref.shape
    rows = ids_ref.shape[1]
    slot = lax.broadcasted_iota(jnp.int32, (slots, rows), 0)
    expert = slot // capacity
    first = expert == ids_ref[0:1, :]
    second = expert == ids_ref[1:2, :]
    named = jnp.where(first | second, 1.0, 0.0)
    before = lax.broadcasted_iota(jnp.int32, (rows, rows), 0) < lax.broadcasted_iota(
        jnp.int32, (rows, rows), 1
    )
    earlier = dot(named.astype(BF16), jnp.where(before, 1.0, 0.0).astype(BF16), NN)
    here = earlier == (slot % capacity).astype(F32)
    first_ref[...] = jnp.where(first & here, 1.0, 0.0).astype(BF16)
    second_ref[...] = jnp.where(second & here, 1.0, 0.0).astype(BF16)
    placing = jnp.where((first | second) & here, 1.0, 0.0).astype(BF16)
    mine = lax.axis_index("xlo") * 2 + lax.axis_index("core")
    sent_ref[...] = dot(placing, tokens_ref[:, columns(mine, quarter)], NN).astype(BF16)


def place_grads(first_ref, second_ref, grads_ref, sent_ref):
    half = sent_ref.shape[1]
    placing = first_ref[...] + second_ref[...]
    mine = lax.axis_index("core")
    sent_ref[...] = dot(placing, grads_ref[:, columns(mine, half)], NN).astype(BF16)


def quarters():
    xlo, core = lax.axis_index("xlo"), lax.axis_index("core")
    return (xlo * 2 + core, (1 - xlo) * 2 + core, xlo * 2 + 1 - core, (1 - xlo) * 2 + 1 - core)


def forward(x0, x1, x2, x3, gate_ref, up_ref, act_ref, pre_ref, hidden_ref):
    quarter = x0.shape[1]
    gate_pre = jnp.zeros(act_ref.shape, F32)
    up_pre = jnp.zeros(act_ref.shape, F32)
    for piece, at in zip((x0, x1, x2, x3), quarters()):
        rows = piece[...]
        gate_pre += dot(rows, gate_ref[0, :, columns(at, quarter)], NT)
        up_pre += dot(rows, up_ref[0, :, columns(at, quarter)], NT)
    activated = gate_pre * jax.nn.sigmoid(gate_pre)
    act_ref[...] = activated
    pre_ref[...] = up_pre * silu_grad(gate_pre)
    hidden_ref[...] = (activated * up_pre).astype(BF16)


def own_hidden_grad(grads_ref, down_ref, out_ref):
    half = grads_ref.shape[1]
    at = lax.axis_index("core")
    out_ref[...] = dot(grads_ref[...], down_ref[0, :, columns(at, half)], NT)


def cotangents(
    own_ref, grads_ref, down_ref, act_ref, pre_ref, hidden_ref, gate_ref, up_ref,
    pre_grad_ref, up_grad_ref, dot_ref, sent_ref,
):
    rows, half = grads_ref.shape
    other = 1 - lax.axis_index("core")
    hidden_grad = own_ref[...] + dot(grads_ref[...], down_ref[0, :, columns(other, half)], NT)
    pre_grad = (hidden_grad * pre_ref[...]).astype(BF16)
    up_grad = (hidden_grad * act_ref[...]).astype(BF16)
    pre_grad_ref[...] = pre_grad
    up_grad_ref[...] = up_grad
    gate_dot = jnp.sum(hidden_ref[...].astype(F32) * hidden_grad, axis=1, keepdims=True)
    dot_ref[...] = jnp.broadcast_to(gate_dot, dot_ref.shape)
    quarter = half // 2
    for i in range(2):
        at = columns(2 * i + other, quarter)
        row_grad = dot(pre_grad, gate_ref[0, :, at], NN) + dot(up_grad, up_ref[0, :, at], NN)
        sent_ref[:, i * quarter : (i + 1) * quarter] = row_grad.astype(BF16)
    sent_ref[:, half:] = in_lanes(three_parts(gate_dot), rows)


def lane_sum(block, start, count):
    lane = lax.broadcasted_iota(jnp.int32, block.shape, 1)
    inside = (lane >= start) & (lane < start + count)
    return jnp.sum(jnp.where(inside, block, 0.0), axis=1, keepdims=True)


def chip_row_grad(pre_grad_ref, up_grad_ref, dot_ref, got_ref, gate_ref, up_ref, out_ref):
    rows, half = out_ref.shape[0], out_ref.shape[1] - LANES
    quarter = half // 2
    pre_grad, up_grad = pre_grad_ref[...], up_grad_ref[...]
    for i in range(2):
        at = columns(2 * i + lax.axis_index("core"), quarter)
        here = slice(i * quarter, (i + 1) * quarter)
        row_grad = dot(pre_grad, gate_ref[0, :, at], NN) + dot(up_grad, up_ref[0, :, at], NN)
        out_ref[:, here] = (row_grad + got_ref[:, here].astype(F32)).astype(BF16)
    gate_dot = dot_ref[:, 0:1] + lane_sum(got_ref[:, half:].astype(F32), 0, 3)
    out_ref[:, half:] = in_lanes(three_parts(gate_dot), rows)


def weight_grads_down(hidden_ref, g0, g1, out_ref):
    half = g0.shape[1]
    at = lax.axis_index("core")
    hidden = hidden_ref[...]
    out_ref[0, :, columns(at, half)] = dot(hidden, g0[...], TN).astype(BF16)
    out_ref[0, :, columns(1 - at, half)] = dot(hidden, g1[...], TN).astype(BF16)


def weight_grads(pre_grad_ref, up_grad_ref, x0, x1, x2, x3, gate_out, up_out):
    quarter = x0.shape[1]
    pre_grad, up_grad = pre_grad_ref[...], up_grad_ref[...]
    for piece, at in zip((x0, x1, x2, x3), quarters()):
        rows = piece[...]
        gate_out[0, :, columns(at, quarter)] = dot(pre_grad, rows, TN).astype(BF16)
        up_out[0, :, columns(at, quarter)] = dot(up_grad, rows, TN).astype(BF16)


def combine(first_ref, second_ref, back_ref, gates_ref, keep_ref, dots_ref, sent_ref):
    rows, quarter = keep_ref.shape
    half = 2 * quarter
    xlo = lax.axis_index("xlo")
    sums = []
    for at in (xlo, 1 - xlo):
        block = back_ref[:, columns(at, quarter)]
        total = gates_ref[:, 0:1] * dot(first_ref[...], block, TN)
        sums.append(total + gates_ref[:, 1:2] * dot(second_ref[...], block, TN))
    keep_ref[...] = sums[0]
    sent_ref[:, :quarter] = sums[1].astype(BF16)
    tail = back_ref[:, half:]
    dots = [lane_sum(dot(which[...], tail, TN), 0, 3) for which in (first_ref, second_ref)]
    lane = lax.broadcasted_iota(jnp.int32, dots_ref.shape, 1)
    dots_ref[...] = jnp.where(lane == 0, dots[0], dots[1])
    sent_ref[:, quarter:] = in_lanes(three_parts(dots[0]) + three_parts(dots[1]), rows)


def finish(keep_ref, dots_ref, got_ref, out_ref, gate_ref):
    quarter = keep_ref.shape[1]
    out_ref[...] = (keep_ref[...] + got_ref[:, :quarter].astype(F32)).astype(BF16)
    tail = got_ref[:, quarter:].astype(F32)
    lane = lax.broadcasted_iota(jnp.int32, gate_ref.shape, 1)
    got = jnp.where(lane == 0, lane_sum(tail, 0, 3), lane_sum(tail, 3, 3))
    gate_ref[...] = dots_ref[...] + got


def body(tokens, grads_out, expert_ids, gates, w_gate, w_up, w_down):
    rows, width = tokens.shape
    hidden_units = w_gate.shape[1]
    experts = lax.axis_size("xhi") * lax.axis_size("z") * lax.axis_size("y")
    capacity = 8
    slots = experts * capacity
    half, quarter = width // 2, width // 4
    swap = [(0, 1), (1, 0)]

    def exchange(value, axis):
        return lax.ppermute(value, axis, swap)

    def to_experts(value):
        shaped = value.reshape(experts, capacity, value.shape[1])
        return lax.all_to_all(shaped, ROWS, split_axis=0, concat_axis=0, tiled=True).reshape(
            value.shape
        )

    unit = 2 * slots * hidden_units * quarter
    sent_x, first, second = call(
        functools.partial(place_tokens, capacity),
        [((slots, quarter), BF16), ((slots, rows), BF16), ((slots, rows), BF16)],
        [expert_ids.T, tokens],
        2 * slots * rows * quarter,
    )
    x0 = to_experts(sent_x)
    (sent_g,) = call(
        place_grads, [((slots, half), BF16)], [first, second, grads_out], 2 * slots * rows * half
    )
    x0, sent_g = lax.optimization_barrier((x0, sent_g))
    g0 = to_experts(sent_g)
    x1 = exchange(x0, "xlo")
    x2 = exchange(x0, "core")
    x3 = exchange(x1, "core")
    act, pre, hidden = call(
        forward,
        [((slots, hidden_units), F32), ((slots, hidden_units), F32), ((slots, hidden_units), BF16)],
        [x0, x1, x2, x3, w_gate, w_up],
        8 * unit,
    )
    act, pre, hidden, g0 = lax.optimization_barrier((act, pre, hidden, g0))
    g1 = exchange(g0, "core")
    (own,) = call(own_hidden_grad, [((slots, hidden_units), F32)], [g0, w_down], 2 * unit)
    pre_grad, up_grad, dots, sent_r = call(
        cotangents,
        [
            ((slots, hidden_units), BF16),
            ((slots, hidden_units), BF16),
            ((slots, LANES), F32),
            ((slots, half + LANES), BF16),
        ],
        [own, g1, w_down, act, pre, hidden, w_gate, w_up],
        6 * unit,
    )
    got_r = exchange(sent_r, "core")
    (row_grad,) = call(
        chip_row_grad,
        [((slots, half + LANES), BF16)],
        [pre_grad, up_grad, dots, got_r, w_gate, w_up],
        4 * unit,
    )
    row_grad, pre_grad, up_grad, hidden = lax.optimization_barrier(
        (row_grad, pre_grad, up_grad, hidden)
    )
    back = to_experts(row_grad)
    (grad_down,) = call(weight_grads_down, [(w_down.shape, BF16)], [hidden, g0, g1], 4 * unit)
    grad_gate, grad_up = call(
        weight_grads,
        [(w_gate.shape, BF16), (w_up.shape, BF16)],
        [pre_grad, up_grad, x0, x1, x2, x3],
        8 * unit,
    )
    keep, token_dots, sent_t = call(
        combine,
        [((rows, quarter), F32), ((rows, 2), F32), ((rows, quarter + LANES), BF16)],
        [first, second, back, gates],
        4 * slots * rows * half,
    )
    got_t = exchange(sent_t, "xlo")
    input_grad, gate_grad = call(
        finish, [((rows, quarter), BF16), ((rows, 2), F32)], [keep, token_dots, got_t], rows * half
    )
    return input_grad, gate_grad, grad_gate, grad_up, grad_down


def solution(mesh):
    dp, wide, narrow = (mesh.shape[name] for name in ("dp", "wide", "narrow"))
    fine = Mesh(
        mesh.devices.reshape(2, dp // 2, 2, wide // 2, narrow), ("xlo", "core", "xhi", "z", "y")
    )
    in_specs = (
        P(ROWS, None),
        P(ROWS, None),
        P(ROWS, None),
        P(ROWS, None),
        P(ROWS, PARTS, None),
        P(ROWS, PARTS, None),
        P(ROWS, PARTS, None),
    )
    out_specs = (
        P(ROWS, PARTS),
        P(ROWS, None),
        P(ROWS, PARTS, None),
        P(ROWS, PARTS, None),
        P(ROWS, PARTS, None),
    )
    return jax.shard_map(body, mesh=fine, in_specs=in_specs, out_specs=out_specs, check_vma=False)
```

time: 511 us -> 224 us (0.44)
  waiting for transfers between devices: 368 us -> 133 us
  Pallas kernels: 0 us -> 45.1 us
  matrix products: 40.8 us -> 0 us
  other arithmetic: 16.1 us -> 0 us
  between operations: 14.2 us -> 0.7 us
  blocking collectives: 13.4 us -> 0 us
  local copies, waits for them, and re-layouts: 21.4 us -> 9.29 us
    all_to_all x4 -> x3, waiting for transfers between devices: 367 us -> 82.3 us  [to_experts(): lax.all_to_all(shaped, ROWS, split_axis=0, concat_axis=0, tiled=True)]
    ppermute x0 -> x6, waiting for transfers between devices: none -> 50.8 us  [exchange(): return lax.ppermute(value, axis, swap)]
    pallas_call x0 -> x10, Pallas kernels: none -> 45.1 us  [call(): pl.pallas_call(kernel, out_shape=[jax.ShapeDtypeStruct(s, t) for s, t in...]
    dot_general x10 -> x0, matrix products: 40.8 us -> none  [the longest x1 5.13 us: body(): jnp.einsum('rd,hd->rh', grad_rows, down_mat, preferred_element_type=jnp.f...]
    gather x4 -> x0, local copies, waits for them, and re-layouts: 17 us -> none  [the longest x2 14.9 us: body(): jnp.take(back_grad, position, axis=0).reshape(tok_rows, TOP, part_width)]
    psum x1 -> x0, blocking collectives: 13.4 us -> none  [body(): gate_grad = lax.psum(token_dots, 'dp')]
    reduce_sum x3 -> x0, other arithmetic: 11.5 us -> none  [the longest x1 11.2 us: body(): token_grad = jnp.sum(pair_rows * gates[:, :, None], axis=1)]
    unnamed x21 -> x22, local copies, waits for them, and re-layouts: 2.33 us -> 9.29 us
  transfers between devices with their start and end apart: 5 -> 9, of which waited for: 5 -> 5; matrix products, arithmetic and copies ran while one was open for 7% -> 0% of each run, Pallas kernels for 0% -> 11%
where the time goes in v1:
time: 224 us; the launch traced here: 223 us
  waiting for transfers between devices  133 us (59%)
  Pallas kernels  45.1 us (20%)
  starting transfers between devices  35.1 us (16%)
  local copies, waits for them, and re-layouts  9.29 us (4%)
    all_to_all x3, waiting for transfers between devices, to_experts(): lax.all_to_all(shaped, ROWS, split_axis=0, concat_axis=0, tiled=True)  82.3 us
    ppermute x6, waiting for transfers between devices, exchange(): return lax.ppermute(value, axis, swap)  50.8 us
    pallas_call x10, Pallas kernels, call(): pl.pallas_call(kernel, out_shape=[jax.ShapeDtypeStruct(s, t) for s, t in...  45.1 us
    all_to_all x3, starting transfers between devices, to_experts(): lax.all_to_all(shaped, ROWS, split_axis=0, concat_axis=0, tiled=True)  33.8 us
    unnamed x22, local copies, waits for them, and re-layouts  9.29 us
  transfers between devices with their start and end apart: 9, of which 5 were waited for; matrix products, arithmetic and copies ran while one was open for 0% of the time, Pallas kernels for 11%

profile of v1, /device:TPU:24, one launch (start us, length us, event | category | flops | bytes accessed | tf_op | source)
XLA Modules:
  0.0 223.3 jit_solution(5607388557151770524)
XLA Ops:
  0.6 2.8 %shard_map.110 = (bf16[512,1024]{1,0:T(8,128)(2,1)}, bf16[512,128]{1,0:T(8,128)(2,1)}, bf16[512,128]{1,0:T(8,128)(2,1)}) custom-call(s32[2,128]{1,0:T(2,128)} %bitcast.18, bf16[128,4096]{1,0:T(8,128)(2,1)} %tokens_ref.1), custom_call_target="tpu_custom_call" | custom-call | flops 134217728 | bytes 2360320 | tf_op jit(solution)/shard_map/pallas_call | solution.py:52
  3.4 14.3 %all-to-all-start = ((bf16[64,8,1024]{2,1,0:T(8,128)(2,1)}), bf16[64,8,1024]{2,1,0:T(8,128)(2,1)S(1)}, u32[]{:S(2)}, u32[]{:S(2)}) async-start(bf16[64,8,1024]{2,1,0:T(8,128)(2,1)} %bitcast.17), calls=%async_computation | async-start | bytes 2097152 | tf_op jit(solution)/shard_map/all_to_all | solution.py:217
  17.8 3.4 %shard_map.111 = bf16[512,2048]{1,0:T(8,128)(2,1)} custom-call(bf16[512,128]{1,0:T(8,128)(2,1)} %get-tuple-element.32.first_ref, bf16[512,128]{1,0:T(8,128)(2,1)} %get-tuple-element.33.second_ref, bf16[128,4096]{1,0:T(8,128)(2,1)} %grads_ref.1), custom_call_target="tpu_custom_call" | custom-call | flops 268435456 | bytes 3407872 | tf_op jit(solution)/shard_map/pallas_call | solution.py:52
  21.1 27.0 %all-to-all-done = bf16[64,8,1024]{2,1,0:T(8,128)(2,1)S(1)} async-done(((bf16[64,8,1024]{2,1,0:T(8,128)(2,1)}), bf16[64,8,1024]{2,1,0:T(8,128)(2,1)S(1)}, u32[]{:S(2)}, u32[]{:S(2)}) %all-to-all-start) | async-done | bytes 1048608 | tf_op jit(solution)/shard_map/all_to_all | solution.py:217
  48.2 0.0 copy-start.3
  48.2 5.8 %all-to-all-start.1 = ((bf16[64,8,2048]{2,1,0:T(8,128)(2,1)}), bf16[64,8,2048]{2,1,0:T(8,128)(2,1)S(1)}, u32[]{:S(2)}, u32[]{:S(2)}) async-start(bf16[64,8,2048]{2,1,0:T(8,128)(2,1)} %bitcast.12), calls=%async_computation.1 | async-start | bytes 4194304 | tf_op jit(solution)/shard_map/all_to_all | solution.py:217
  54.0 0.7 collective-permute-start
  54.7 0.0 copy-done.3
  54.7 0.0 collective-permute-start.1
  54.7 43.8 %collective-permute-done.x1 = bf16[512,1024]{1,0:T(8,128)(2,1)S(1)} collective-permute-done((bf16[512,1024]{1,0:T(8,128)(2,1)S(1)}, bf16[512,1024]{1,0:T(8,128)(2,1)S(1)}, u32[]{:S(2)}, u32[]{:S(2)}) %collective-permute-start) | collective-permute-done | bytes 1048608 | tf_op jit(solution)/shard_map/ppermute | solution.py:213
  98.5 0.0 copy-start.5
  98.5 0.0 collective-permute-start.2
  98.5 0.0 collective-permute-done.1.x2
  98.5 0.0 copy-start.6
  98.5 2.6 %collective-permute-done.2.x3 = bf16[512,1024]{1,0:T(8,128)(2,1)S(1)} collective-permute-done((bf16[512,1024]{1,0:T(8,128)(2,1)S(1)}, bf16[512,1024]{1,0:T(8,128)(2,1)S(1)}, u32[]{:S(2)}, u32[]{:S(2)}) %collective-permute-start.2) | collective-permute-done | bytes 1048608 | tf_op jit(solution)/shard_map/ppermute | solution.py:213
  101.1 0.0 copy-done.5
  101.1 0.0 copy-done.6
  101.1 0.0 copy-start.7
  101.1 1.0 copy-done.7
  102.1 6.6 %shard_map.112 = (f32[512,192]{1,0:T(8,128)}, f32[512,192]{1,0:T(8,128)}, bf16[512,192]{1,0:T(8,128)(2,1)}) custom-call(bf16[512,1024]{1,0:T(8,128)(2,1)} %bitcast.15, bf16[512,1024]{1,0:T(8,128)(2,1)} %copy-done.5, bf16[512,1024]{1,0:T(8,128)(2,1)} %copy-done.6, bf16[512,1024]{1,0:T(8,128)(2,1)} %copy-done.7, bf16[1,192,4096]{2,1,0:T(8,128)(2,1)} %gate_ref.5, ...), custom_call_target="tpu_custom_call" | custom-call | flops 1610612736 | bytes 8323072 | tf_op jit(solution)/shard_map/pallas_call | solution.py:52
  108.7 0.0 all-to-all-done.1
  108.7 0.0 copy-start
  108.7 0.2 collective-permute-start.3
  109.0 1.2 copy-done
  110.1 3.6 %shard_map.113.own_ref = f32[512,192]{1,0:T(8,128)} custom-call(bf16[512,2048]{1,0:T(8,128)(2,1)} %bitcast.8, bf16[1,192,4096]{2,1,0:T(8,128)(2,1)} %down_ref.3), custom_call_target="tpu_custom_call" | custom-call | flops 402653184 | bytes 4063232 | tf_op jit(solution)/shard_map/pallas_call | solution.py:52
  113.7 0.0 collective-permute-done.3.grads_ref.g1
  113.7 0.0 copy-start.2
  113.7 1.4 copy-done.2
  115.1 7.8 %shard_map.114 = (bf16[512,192]{1,0:T(8,128)(2,1)}, bf16[512,192]{1,0:T(8,128)(2,1)}, f32[512,128]{1,0:T(8,128)}, bf16[512,2176]{1,0:T(8,128)(2,1)}) custom-call(f32[512,192]{1,0:T(8,128)} %shard_map.113.own_ref, bf16[512,2048]{1,0:T(8,128)(2,1)} %copy-done.2, bf16[1,192,4096]{2,1,0:T(8,128)(2,1)} %down_ref.3, f32[512,192]{1,0:T(8,128)} %get-tuple-element.41.act_ref, ...), custom_call_target="tpu_custom_call" | custom-call | flops 1207959552 | bytes 11075584 | tf_op jit(solution)/shard_map/pallas_call | solution.py:52
  122.9 0.1 collective-permute-start.4
  123.1 4.4 %collective-permute-done.4.got_ref = bf16[512,2176]{1,0:T(8,128)(2,1)S(1)} collective-permute-done((bf16[512,2176]{1,0:T(8,128)(2,1)}, bf16[512,2176]{1,0:T(8,128)(2,1)S(1)}, u32[]{:S(2)}, u32[]{:S(2)}) %collective-permute-start.4) | collective-permute-done | bytes 2228256 | tf_op jit(solution)/shard_map/ppermute | solution.py:213
  127.5 0.0 copy-start.4
  127.5 1.4 copy-done.4
  128.9 5.4 %shard_map.115 = bf16[512,2176]{1,0:T(8,128)(2,1)} custom-call(bf16[512,192]{1,0:T(8,128)(2,1)} %get-tuple-element.54.pre_grad_ref, bf16[512,192]{1,0:T(8,128)(2,1)} %get-tuple-element.55.up_grad_ref, f32[512,128]{1,0:T(8,128)} %get-tuple-element.46.dot_ref, bf16[512,2176]{1,0:T(8,128)(2,1)} %copy-done.4, bf16[1,192,4096]{2,1,0:T(8,128)(2,1)} %gate_ref.5, ...), custom_call_target="tpu_custom_call" | custom-call | flops 805306368 | bytes 8257536 | tf_op jit(solution)/shard_map/pallas_call | solution.py:52
  134.3 0.0 copy-start.9
  134.3 13.6 %all-to-all-start.2 = ((bf16[64,8,2176]{2,1,0:T(8,128)(2,1)}), bf16[64,8,2176]{2,1,0:T(8,128)(2,1)S(1)}, u32[]{:S(2)}, u32[]{:S(2)}) async-start(bf16[64,8,2176]{2,1,0:T(8,128)(2,1)} %bitcast.11), calls=%async_computation.2 | async-start | bytes 4456448 | tf_op jit(solution)/shard_map/all_to_all | solution.py:217
  148.0 0.0 copy-done.9
  148.0 0.7 copy.12.gates_ref
  148.7 55.2 %all-to-all-done.2 = bf16[64,8,2176]{2,1,0:T(8,128)(2,1)S(1)} async-done(((bf16[64,8,2176]{2,1,0:T(8,128)(2,1)}), bf16[64,8,2176]{2,1,0:T(8,128)(2,1)S(1)}, u32[]{:S(2)}, u32[]{:S(2)}) %all-to-all-start.2) | async-done | bytes 2228256 | tf_op jit(solution)/shard_map/all_to_all | solution.py:217
  204.0 1.4 copy-done.1
  205.3 3.4 %shard_map.116 = (f32[128,1024]{1,0:T(8,128)}, f32[128,2]{1,0:T(8,128)}, bf16[128,1152]{1,0:T(8,128)(2,1)}) custom-call(bf16[512,128]{1,0:T(8,128)(2,1)} %get-tuple-element.32.first_ref, bf16[512,128]{1,0:T(8,128)(2,1)} %get-tuple-element.33.second_ref, bf16[512,2176]{1,0:T(8,128)(2,1)} %bitcast.10, f32[128,2]{1,0:T(8,128)} %copy.12.gates_ref), custom_call_target="tpu_custom_call" | custom-call | flops 536870912 | bytes 3311616 | tf_op jit(solution)/shard_map/pallas_call | solution.py:52
  208.8 0.2 collective-permute-start.5
  209.0 4.5 %shard_map.119 = bf16[1,192,4096]{2,1,0:T(8,128)(2,1)} custom-call(bf16[512,192]{1,0:T(8,128)(2,1)} %get-tuple-element.58.hidden_ref, bf16[512,2048]{1,0:T(8,128)(2,1)} %bitcast.9, bf16[512,2048]{1,0:T(8,128)(2,1)} %copy-done.2), custom_call_target="tpu_custom_call" | custom-call | flops 805306368 | bytes 5963776 | tf_op jit(solution)/shard_map/pallas_call | solution.py:52
  213.4 5.6 %shard_map.118 = (bf16[1,192,4096]{2,1,0:T(8,128)(2,1)}, bf16[1,192,4096]{2,1,0:T(8,128)(2,1)}) custom-call(bf16[512,192]{1,0:T(8,128)(2,1)} %get-tuple-element.54.pre_grad_ref, bf16[512,192]{1,0:T(8,128)(2,1)} %get-tuple-element.55.up_grad_ref, bf16[512,1024]{1,0:T(8,128)(2,1)} %bitcast.16, bf16[512,1024]{1,0:T(8,128)(2,1)} %copy-done.5, ...), custom_call_target="tpu_custom_call" | custom-call | flops 1610612736 | bytes 7733248 | tf_op jit(solution)/shard_map/pallas_call | solution.py:52
  219.1 0.0 collective-permute-done.5.got_ref
  219.1 0.7 copy-done.8
  219.8 2.0 shard_map.117
  221.8 1.5 copy.13
  (2 shorter events, 0.0 us)
Async XLA Ops:
  3.4 44.8 %all-to-all-start = ((bf16[64,8,1024]{2,1,0:T(8,128)(2,1)}), bf16[64,8,1024]{2,1,0:T(8,128)(2,1)S(1)}, u32[]{:S(2)}, u32[]{:S(2)}) async-start(bf16[64,8,1024]{2,1,0:T(8,128)(2,1)} %bitcast.17), calls=%async_computation | async-start | bytes 2097152 | tf_op jit(solution)/shard_map/all_to_all | solution.py:217
  48.2 6.5 %copy-start.3 = (bf16[64,8,1024]{2,1,0:T(8,128)(2,1)}, bf16[64,8,1024]{2,1,0:T(8,128)(2,1)S(1)}, u32[]{:S(2)}) copy-start(bf16[64,8,1024]{2,1,0:T(8,128)(2,1)S(1)} %all-to-all-done) | copy-start | bytes 3145732
  48.2 60.6 %all-to-all-start.1 = ((bf16[64,8,2048]{2,1,0:T(8,128)(2,1)}), bf16[64,8,2048]{2,1,0:T(8,128)(2,1)S(1)}, u32[]{:S(2)}, u32[]{:S(2)}) async-start(bf16[64,8,2048]{2,1,0:T(8,128)(2,1)} %bitcast.12), calls=%async_computation.1 | async-start | bytes 4194304 | tf_op jit(solution)/shard_map/all_to_all | solution.py:217
  54.0 44.5 %collective-permute-start = (bf16[512,1024]{1,0:T(8,128)(2,1)S(1)}, bf16[512,1024]{1,0:T(8,128)(2,1)S(1)}, u32[]{:S(2)}, u32[]{:S(2)}) collective-permute-start(bf16[512,1024]{1,0:T(8,128)(2,1)S(1)} %bitcast.13), channel_id=1, source_target_pairs={{0,128},{128,0},{1,129},{129,1},{2,130},{130,2},{3,131},{131,3},{4... | collective-permute-start | bytes 3145736 | tf_op jit(solution)/shard_map/ppermute | solution.py:213
  54.7 43.8 %collective-permute-start.1 = (bf16[512,1024]{1,0:T(8,128)(2,1)S(1)}, bf16[512,1024]{1,0:T(8,128)(2,1)S(1)}, u32[]{:S(2)}, u32[]{:S(2)}) collective-permute-start(bf16[512,1024]{1,0:T(8,128)(2,1)S(1)} %bitcast.14), channel_id=1, source_target_pairs={{0,64},{64,0},{1,65},{65,1},{2,66},{66,2},{3,67},{67,3},{4,68},{68... | collective-permute-start | bytes 3145736 | tf_op jit(solution)/shard_map/ppermute | solution.py:213
  98.5 2.7 %copy-start.5 = (bf16[512,1024]{1,0:T(8,128)(2,1)}, bf16[512,1024]{1,0:T(8,128)(2,1)S(1)}, u32[]{:S(2)}) copy-start(bf16[512,1024]{1,0:T(8,128)(2,1)S(1)} %collective-permute-done.x1) | copy-start | bytes 3145732
  98.5 2.7 %collective-permute-start.2 = (bf16[512,1024]{1,0:T(8,128)(2,1)S(1)}, bf16[512,1024]{1,0:T(8,128)(2,1)S(1)}, u32[]{:S(2)}, u32[]{:S(2)}) collective-permute-start(bf16[512,1024]{1,0:T(8,128)(2,1)S(1)} %collective-permute-done.x1), channel_id=1, source_target_pairs={{0,64},{64,0},{1,65},{65,1},{2,66},{66,2},{3,67},{67,3},{4,68},{68... | collective-permute-start | bytes 3145736 | tf_op jit(solution)/shard_map/ppermute | solution.py:213
  98.5 2.7 %copy-start.6 = (bf16[512,1024]{1,0:T(8,128)(2,1)}, bf16[512,1024]{1,0:T(8,128)(2,1)S(1)}, u32[]{:S(2)}) copy-start(bf16[512,1024]{1,0:T(8,128)(2,1)S(1)} %collective-permute-done.1.x2) | copy-start | bytes 3145732
  101.1 1.0 copy-start.7
  108.7 1.4 copy-start
  108.7 5.0 %collective-permute-start.3 = (bf16[512,2048]{1,0:T(8,128)(2,1)S(1)}, bf16[512,2048]{1,0:T(8,128)(2,1)S(1)}, u32[]{:S(2)}, u32[]{:S(2)}) collective-permute-start(bf16[512,2048]{1,0:T(8,128)(2,1)S(1)} %bitcast.7), channel_id=1, source_target_pairs={{0,64},{64,0},{1,65},{65,1},{2,66},{66,2},{3,67},{67,3},{4,68},{68... | collective-permute-start | bytes 6291464 | tf_op jit(solution)/shard_map/ppermute | solution.py:213
  113.7 1.4 copy-start.2
  122.9 4.6 %collective-permute-start.4 = (bf16[512,2176]{1,0:T(8,128)(2,1)}, bf16[512,2176]{1,0:T(8,128)(2,1)S(1)}, u32[]{:S(2)}, u32[]{:S(2)}) collective-permute-start(bf16[512,2176]{1,0:T(8,128)(2,1)} %get-tuple-element.47), channel_id=1, source_target_pairs={{0,64},{64,0},{1,65},{65,1},{2,66},{66,2},{3,67},{67,3},{4,68},{68... | collective-permute-start | bytes 6684680 | tf_op jit(solution)/shard_map/ppermute | solution.py:213
  127.5 1.4 copy-start.4
  134.3 13.7 %copy-start.9 = (f32[128,2]{0,1:T(2,128)S(1)}, f32[128,2]{0,1:T(2,128)}, u32[]{:S(2)}) copy-start(f32[128,2]{0,1:T(2,128)} %param.10) | copy-start | bytes 3076
  134.3 69.7 %all-to-all-start.2 = ((bf16[64,8,2176]{2,1,0:T(8,128)(2,1)}), bf16[64,8,2176]{2,1,0:T(8,128)(2,1)S(1)}, u32[]{:S(2)}, u32[]{:S(2)}) async-start(bf16[64,8,2176]{2,1,0:T(8,128)(2,1)} %bitcast.11), calls=%async_computation.2 | async-start | bytes 4456448 | tf_op jit(solution)/shard_map/all_to_all | solution.py:217
  204.0 1.4 copy-start.1
  208.8 10.3 %collective-permute-start.5 = (bf16[128,1152]{1,0:T(8,128)(2,1)}, bf16[128,1152]{1,0:T(8,128)(2,1)S(1)}, u32[]{:S(2)}, u32[]{:S(2)}) collective-permute-start(bf16[128,1152]{1,0:T(8,128)(2,1)} %get-tuple-element.51), channel_id=1, source_target_pairs={{0,128},{128,0},{1,129},{129,1},{2,130},{130,2},{3,131},{131,3},{4... | collective-permute-start | bytes 884744 | tf_op jit(solution)/shard_map/ppermute | solution.py:213
  219.1 0.7 copy-start.8

commit v2 on v0

v2 whole, which is shorter than its diff:
```python
import itertools
import math

import jax
import jax.numpy as jnp
from jax import lax
from jax.experimental import pallas as pl
from jax.experimental.pallas import tpu as pltpu
from jax.sharding import Mesh, PartitionSpec as P

F32 = jnp.float32
BF16 = jnp.bfloat16
LANES = 128
TAIL = 16
CAPACITY = 8
MIB = 1024 * 1024
VMEM_LIMIT = 60 * MIB
ROWS = ("xhi", "z", "y")
PARTS = ("xlo", "core")
ALL = PARTS + ROWS
NN = ((1,), (0,))
NT = ((1,), (1,))
TN = ((0,), (0,))


def dot(a, b, dims):
    return lax.dot_general(a, b, (dims, ((), ())), preferred_element_type=F32)


def three_parts(value):
    high = value.astype(BF16).astype(F32)
    rest = value - high
    middle = rest.astype(BF16).astype(F32)
    return high, middle, (rest - middle).astype(BF16).astype(F32)


def in_rows(parts, height):
    row = lax.broadcasted_iota(jnp.int32, (height, parts[0].shape[1]), 0)
    block = jnp.zeros(row.shape, F32)
    for i, part in enumerate(parts):
        block = jnp.where(row == i, part, block)
    return block


class Copies:
    def __init__(self, sems):
        self.sems, self.used = sems, 0

    def start(self, source, target):
        copy = pltpu.make_async_copy(source, target, self.sems.at[self.used])
        self.used += 1
        copy.start()
        return copy


def call(kernel, outs, args, scratch, copies, flops, vmem=VMEM_LIMIT):
    moved = sum(a.size * a.dtype.itemsize for a in args)
    moved += sum(math.prod(s) * jnp.dtype(t).itemsize for s, t in outs)
    place = pl.BlockSpec(memory_space=pl.ANY)
    return pl.pallas_call(
        kernel,
        out_shape=[jax.ShapeDtypeStruct(s, t) for s, t in outs],
        in_specs=[place] * len(args),
        out_specs=[place] * len(outs),
        scratch_shapes=[pltpu.VMEM(s, t) for s, t in scratch] + [pltpu.SemaphoreType.DMA((copies,))],
        compiler_params=pltpu.CompilerParams(vmem_limit_bytes=vmem),
        cost_estimate=pl.CostEstimate(flops=flops, bytes_accessed=moved, transcendentals=0),
    )(*args)


def columns(block, width, start=0):
    return pl.ds(pl.multiple_of(start + block * width, LANES), width)


def xlo():
    return lax.axis_index("xlo")


def core():
    return lax.axis_index("core")


def side():
    return lax.bitwise_xor(lax.axis_index("xlo"), lax.axis_index("xhi"))


def piece_order():
    near, far, mine, other = side(), 1 - side(), core(), 1 - core()
    return (near * 2 + mine, far * 2 + mine, near * 2 + other, far * 2 + other)


def choices(ids, slots):
    rows = ids.shape[1]
    slot = lax.broadcasted_iota(jnp.int32, (slots, rows), 0)
    expert = slot // CAPACITY
    first, second = expert == ids[0:1, :], expert == ids[1:2, :]
    before = lax.broadcasted_iota(jnp.int32, (rows, rows), 0) < lax.broadcasted_iota(
        jnp.int32, (rows, rows), 1
    )
    named = jnp.where(first | second, 1.0, 0.0).astype(BF16)
    earlier = dot(named, jnp.where(before, 1.0, 0.0).astype(BF16), NN)
    here = earlier == (slot % CAPACITY).astype(F32)
    return jnp.where(first & here, 1.0, 0.0), jnp.where(second & here, 1.0, 0.0)


def write_parts(copies, placing, rows, sent, sent_hbm, start, stop, step):
    out = []
    for at in range(start, stop, step):
        part = slice(at, at + step)
        sent[:, part] = dot(placing, rows[:, at - start : at - start + step], NN).astype(BF16)
        out.append(copies.start(sent.at[:, part], sent_hbm.at[:, part]))
    return out


def place_first(ids_hbm, x_hbm, g_hbm, sent_hbm, ids, x, g, sent, sems):
    copies = Copies(sems)
    quarter, eighth = x.shape[1], g.shape[1]
    block = side() * 2 + core()
    got_ids = copies.start(ids_hbm, ids)
    got_x = copies.start(x_hbm.at[:, columns(block, quarter)], x)
    got_g = copies.start(g_hbm.at[:, columns(block, eighth)], g)
    got_ids.wait()
    first, second = choices(ids[...], sent.shape[0])
    placing = (first + second).astype(BF16)
    got_x.wait()
    out = write_parts(copies, placing, x, sent, sent_hbm, 0, quarter, eighth)
    got_g.wait()
    out += write_parts(copies, placing, g, sent, sent_hbm, quarter, quarter + eighth, eighth)
    for copy in out:
        copy.wait()


def place_second(ids_hbm, g_hbm, sent_hbm, ids, g, sent, sems):
    copies = Copies(sems)
    quarter = g.shape[1]
    got_ids = copies.start(ids_hbm, ids)
    got_g = copies.start(g_hbm.at[:, columns(core(), quarter, 2 * quarter)], g)
    got_ids.wait()
    first, second = choices(ids[...], sent.shape[0])
    placing = (first + second).astype(BF16)
    got_g.wait()
    for copy in write_parts(copies, placing, g, sent, sent_hbm, 0, quarter, quarter // 2):
        copy.wait()


def split(both_hbm, x_hbm, g_hbm, x, g, sems):
    copies = Copies(sems)
    parts = 4
    rows, width = x.shape[0] // parts, x.shape[1]
    got = []
    for held, at in ((x, pl.ds(0, width)), (g, pl.ds(width, g.shape[1]))):
        for i in range(parts):
            here = slice(i * rows, (i + 1) * rows)
            got.append(copies.start(both_hbm.at[here, at], held.at[here]))
    sent = []
    for j, (held, out) in enumerate(((x, x_hbm), (g, g_hbm))):
        for i in range(parts):
            here = slice(i * rows, (i + 1) * rows)
            got[j * parts + i].wait()
            sent.append(copies.start(held.at[here], out.at[here]))
    for copy in sent:
        copy.wait()


def pick(ids_hbm, first_hbm, second_hbm, ids, first, second, sems):
    copies = Copies(sems)
    copies.start(ids_hbm, ids).wait()
    values = choices(ids[...], first.shape[1])
    first[...] = jnp.transpose(values[0]).astype(BF16)
    second[...] = jnp.transpose(values[1]).astype(BF16)
    out = [copies.start(first, first_hbm), copies.start(second, second_hbm)]
    for copy in out:
        copy.wait()


def share_far(gate_hbm, up_hbm, far_both, both, sems):
    copies = Copies(sems)
    units, half = both.shape[0] // 2, both.shape[1]
    got = []
    for i, ref in enumerate((gate_hbm, up_hbm)):
        there = slice(i * units, (i + 1) * units)
        got.append(copies.start(ref.at[0, :, columns(1 - xlo(), half)], both.at[there]))
    sent = []
    for i in range(2):
        there = slice(i * units, (i + 1) * units)
        got[i].wait()
        sent.append(copies.start(both.at[there], far_both.at[there]))
    for copy in sent:
        copy.wait()


def share_near(gate_hbm, up_hbm, down_hbm, near_both, near_down, both, down, sems):
    copies = Copies(sems)
    units, quarter = both.shape[0] // 2, both.shape[1]
    eighth, other = quarter // 2, 1 - core()
    got = []
    for i, ref in enumerate((gate_hbm, up_hbm)):
        there = both.at[i * units : (i + 1) * units]
        got.append(copies.start(ref.at[0, :, columns(xlo() * 2 + other, quarter)], there))
    for i in range(2):
        there = down.at[:, i * eighth : (i + 1) * eighth]
        got.append(copies.start(down_hbm.at[0, :, columns(2 * i + other, eighth)], there))
    direct = down_hbm.at[0, :, columns(other, quarter, 2 * quarter)]
    got.append(copies.start(direct, down.at[:, quarter:]))
    for copy in got:
        copy.wait()
    sent = [copies.start(both, near_both), copies.start(down, near_down)]
    for copy in sent:
        copy.wait()


def pass_on(both_hbm, out_hbm, both, sems):
    copies = Copies(sems)
    copies.start(both_hbm.at[:, columns(1 - core(), both.shape[1])], both).wait()
    copies.start(both, out_hbm).wait()


def forward(x0, x1, x2, x3, gate_hbm, up_hbm, act_hbm, pre_hbm, hidden_hbm, *scratch):
    x, gate, up, act, pre, hidden, sems = scratch
    copies = Copies(sems)
    quarter = x.shape[2]
    started = []
    for i, (ref, at) in enumerate(zip((x0, x1, x2, x3), piece_order())):
        started.append(
            [
                copies.start(ref, x.at[i]),
                copies.start(gate_hbm.at[0, :, columns(at, quarter)], gate.at[i]),
                copies.start(up_hbm.at[0, :, columns(at, quarter)], up.at[i]),
            ]
        )
    gate_pre = jnp.zeros(act.shape, F32)
    up_pre = jnp.zeros(act.shape, F32)
    for i in range(4):
        for copy in started[i]:
            copy.wait()
        gate_pre += dot(gate[i], x[i], NT)
        up_pre += dot(up[i], x[i], NT)
    sig = jax.nn.sigmoid(gate_pre)
    activated = gate_pre * sig
    act[...] = activated
    pre[...] = up_pre * (sig * (1.0 + gate_pre * (1.0 - sig)))
    hidden[...] = (activated * up_pre).astype(BF16)
    out = [copies.start(a, b) for a, b in ((act, act_hbm), (pre, pre_hbm), (hidden, hidden_hbm))]
    for copy in out:
        copy.wait()


def hidden_grads(g0, g1, gd, down_hbm, near_hbm, mine_hbm, theirs_hbm, g, down, total, sems):
    copies = Copies(sems)
    units = down.shape[0] // 2
    quarter = g.shape[1] // 2
    eighth = quarter // 2
    parts = (slice(0, eighth), slice(eighth, quarter), slice(quarter, 2 * quarter))
    near, far = piece_order()[:2]
    own = (columns(near, eighth), columns(far, eighth), columns(core(), quarter, 2 * quarter))
    theirs = (columns(side(), eighth), columns(1 - side(), eighth), pl.ds(quarter, quarter))
    got = [
        [
            copies.start(ref, g.at[:, part]),
            copies.start(near_hbm.at[:, a], down.at[:units, part]),
            copies.start(down_hbm.at[0, :, b], down.at[units:, part]),
        ]
        for ref, part, a, b in zip((g0, g1, gd), parts, theirs, own)
    ]
    sums = jnp.zeros(total.shape, F32)
    for copy_list, part in zip(got, parts):
        for copy in copy_list:
            copy.wait()
        sums += dot(down[:, part], g[:, part], NT)
    total[...] = sums
    out = [copies.start(total.at[:units], theirs_hbm), copies.start(total.at[units:], mine_hbm)]
    for copy in out:
        copy.wait()


def cotangents(mine_hbm, got_hbm, act_hbm, pre_hbm, hidden_hbm, pack_hbm, *scratch):
    mine, got, act, pre, hidden, pack, sems = scratch
    copies = Copies(sems)
    units = mine.shape[0]
    pairs = ((mine_hbm, mine), (got_hbm, got), (pre_hbm, pre), (act_hbm, act), (hidden_hbm, hidden))
    started = [copies.start(a, b) for a, b in pairs]
    for copy in started:
        copy.wait()
    hidden_grad = mine[...] + got[...]
    pack[:units] = (hidden_grad * pre[...]).astype(BF16)
    pack[units : 2 * units] = (hidden_grad * act[...]).astype(BF16)
    gate_dot = jnp.sum(hidden[...].astype(F32) * hidden_grad, axis=0, keepdims=True)
    pack[2 * units :] = in_rows(three_parts(gate_dot), TAIL).astype(BF16)
    copies.start(pack, pack_hbm).wait()


def near_row_grad(own_hbm, near_hbm, gate_hbm, up_hbm, both_hbm, out_hbm, *scratch):
    own, near, mine, both, total, sems = scratch
    copies = Copies(sems)
    units, quarter = mine.shape[0] // 2, mine.shape[1]
    at = columns(xlo() * 2 + core(), quarter)
    started = [
        copies.start(own_hbm, own),
        copies.start(gate_hbm.at[0, :, at], mine.at[:units]),
        copies.start(up_hbm.at[0, :, at], mine.at[units:]),
        copies.start(near_hbm, near),
        copies.start(both_hbm, both),
    ]
    for copy in started:
        copy.wait()
    total[...] = dot(own[: 2 * units], mine[...], TN) + dot(near[: 2 * units], both[...], TN)
    copies.start(total, out_hbm).wait()


def row_grad(
    begun_hbm, own_hbm, near_hbm, far_hbm, last_hbm, far_both, last_both, out_hbm, *scratch
):
    total, own, near, far, last, wide, lasting, sent, sems = scratch
    copies = Copies(sems)
    units2, quarter = wide.shape
    pairs = (
        (far_hbm, far),
        (far_both.at[:, columns(core(), quarter)], wide),
        (last_hbm, last),
        (last_both, lasting),
        (begun_hbm, total),
        (own_hbm.at[units2:], own),
        (near_hbm.at[units2:], near),
    )
    started = [copies.start(a, b) for a, b in pairs]
    started[0].wait()
    far_rows = jnp.transpose(far[:units2])
    started[1].wait()
    started[2].wait()
    last_rows = jnp.transpose(last[:units2])
    started[5].wait()
    started[6].wait()
    tails = own[...].astype(F32) + near[...].astype(F32)
    tails += far[units2:].astype(F32) + last[units2:].astype(F32)
    gate_dot = jnp.sum(tails, axis=0, keepdims=True)
    sent[:, quarter:] = jnp.transpose(in_rows(three_parts(gate_dot), LANES)).astype(BF16)
    started[3].wait()
    started[4].wait()
    out = []
    for i in range(2):
        part = slice(i * (quarter // 2), (i + 1) * (quarter // 2))
        sums = dot(far_rows, wide[:, part], NN) + dot(last_rows, lasting[:, part], NN)
        sent[:, part] = (total[:, part] + sums).astype(BF16)
        if i:
            part = slice(quarter // 2, quarter + LANES)
        out.append(copies.start(sent.at[:, part], out_hbm.at[:, part]))
    for copy in out:
        copy.wait()


def weight_grads(pack_hbm, x0, x1, x2, x3, gate_hbm, up_hbm, pack, x, out, sems):
    copies = Copies(sems)
    units, quarter = out.shape[1] // 2, x.shape[2]
    got = [copies.start(pack_hbm.at[: 2 * units], pack)]
    got += [copies.start(ref, x.at[i]) for i, ref in enumerate((x0, x1, x2, x3))]
    got[0].wait()
    sent = []
    for i, at in enumerate(piece_order()):
        got[i + 1].wait()
        out[i] = dot(pack[...], x[i], NN).astype(BF16)
        there = columns(at, quarter)
        sent.append(copies.start(out.at[i, :units], gate_hbm.at[0, :, there]))
        sent.append(copies.start(out.at[i, units:], up_hbm.at[0, :, there]))
    for copy in sent:
        copy.wait()


def weight_grads_down(hidden_hbm, g0, g1, g2, g3, gd0, gd1, down_hbm, *scratch):
    hidden, g, gd, out, direct, sems = scratch
    copies = Copies(sems)
    eighth = g.shape[2]
    got = [copies.start(hidden_hbm, hidden)]
    got += [copies.start(ref, g.at[i]) for i, ref in enumerate((g0, g1, g2, g3))]
    got += [copies.start(ref, gd.at[i]) for i, ref in enumerate((gd0, gd1))]
    got[0].wait()
    sent = []
    for i, at in enumerate(piece_order()):
        got[i + 1].wait()
        out[i] = dot(hidden[...], g[i], NN).astype(BF16)
        sent.append(copies.start(out.at[i], down_hbm.at[0, :, columns(at, eighth)]))
    for i, at in enumerate((core(), 1 - core())):
        got[i + 5].wait()
        direct[i] = dot(hidden[...], gd[i], NN).astype(BF16)
        there = columns(at, 2 * eighth, 4 * eighth)
        sent.append(copies.start(direct.at[i], down_hbm.at[0, :, there]))
    for copy in sent:
        copy.wait()


def combine(first_hbm, second_hbm, back_hbm, gates_hbm, out_hbm, dots_hbm, *scratch):
    first, second, back, gates, out, dots, sems = scratch
    copies = Copies(sems)
    rows, quarter = out.shape
    parts = (slice(0, quarter // 2), slice(quarter // 2, quarter + LANES))
    pairs = ((gates_hbm, gates), (first_hbm, first), (second_hbm, second))
    started = [copies.start(a, b) for a, b in pairs]
    got = [copies.start(back_hbm.at[:, part], back.at[:, part]) for part in parts]
    for copy in started:
        copy.wait()
    weights = jnp.transpose(in_rows((gates[0:1, :], gates[1:2, :]), LANES))
    sent = []
    for i, part in enumerate(parts):
        got[i].wait()
        picked = [dot(ref[...], back[:, part], NN) for ref in (first, second)]
        total = weights[:, 0:1] * picked[0] + weights[:, 1:2] * picked[1]
        there = slice(i * (quarter // 2), (i + 1) * (quarter // 2))
        out[:, there] = total[:, : quarter // 2].astype(BF16)
        sent.append(copies.start(out.at[:, there], out_hbm.at[:, there]))
    lane = lax.broadcasted_iota(jnp.int32, (rows, LANES), 1)
    for i in range(2):
        tail = jnp.transpose(jnp.where(lane < 3, picked[i][:, quarter // 2 :], 0.0))
        dots[i : i + 1, :] = jnp.sum(tail, axis=0, keepdims=True)
    sent.append(copies.start(dots, dots_hbm))
    for copy in sent:
        copy.wait()


def crossing_groups(sizes):
    xhi, z, y = sizes
    groups = []
    for start, one in itertools.product(range(2), range(2)):
        groups.append(
            [
                ((((start ^ h) * 2 + one) * xhi + h) * z + i) * y + j
                for h, i, j in itertools.product(range(xhi), range(z), range(y))
            ]
        )
    return groups


def body(tokens, grads_out, expert_ids, gates, w_gate, w_up, w_down):
    rows, width = tokens.shape
    units = w_gate.shape[1]
    sizes = tuple(lax.axis_size(name) for name in ROWS)
    experts = sizes[0] * sizes[1] * sizes[2]
    slots = experts * CAPACITY
    quarter, half = width // 4, width // 2
    groups = crossing_groups(sizes)

    def exchange(value, axis):
        return lax.ppermute(value, axis, [(0, 1), (1, 0)])

    def to_experts(value):
        shaped = value.reshape(experts, CAPACITY, value.shape[1])
        moved = lax.all_to_all(
            shaped, ALL, split_axis=0, concat_axis=0, tiled=True, axis_index_groups=groups
        )
        return moved.reshape(value.shape)

    def to_tokens(value):
        shaped = value.reshape(experts, CAPACITY, value.shape[1])
        moved = lax.all_to_all(shaped, ROWS, split_axis=0, concat_axis=0, tiled=True)
        return moved.reshape(value.shape)

    unit = 2 * slots * units * quarter
    eighth = width // 8
    ids, gates = expert_ids.T, gates.T
    piece, wide, tall = ((slots, quarter), BF16), ((units, slots), F32), ((2 * units, quarter), BF16)
    pack = ((2 * units + TAIL, slots), BF16)
    hidden_type = ((units, slots), BF16)
    half_down = ((units, half), BF16)
    id_type, chosen = ((2, rows), jnp.int32), ((rows, slots), BF16)

    (sent_first,) = call(
        place_first,
        [((slots, quarter + eighth), BF16)],
        [ids, tokens, grads_out],
        [
            id_type,
            ((rows, quarter), BF16),
            ((rows, eighth), BF16),
            ((slots, quarter + eighth), BF16),
        ],
        6,
        unit // 2,
    )
    got_first = to_experts(sent_first)
    shared = ((2 * units, half), BF16)
    (far_both,) = call(share_far, [shared], [w_gate, w_up], [shared], 4, 1000)
    far_both = exchange(far_both, "xlo")
    near_both, near_down = call(
        share_near, [tall, half_down], [w_gate, w_up, w_down], [tall, half_down], 7, 1000
    )
    near_both, near_down = exchange(near_both, "core"), exchange(near_down, "core")
    (sent_second,) = call(
        place_second,
        [piece],
        [ids, grads_out],
        [id_type, ((rows, quarter), BF16), piece],
        4,
        unit // 2,
    )
    first, second = call(pick, [chosen, chosen], [ids], [id_type, chosen, chosen], 3, unit // 4)
    got_first, sent_second, first, second, near_both, near_down, far_both = (
        lax.optimization_barrier(
            (got_first, sent_second, first, second, near_both, near_down, far_both)
        )
    )
    eighth_piece = ((slots, eighth), BF16)
    x0, g0 = call(
        split, [piece, eighth_piece], [got_first], [piece, eighth_piece], 16, 1000, 8 * MIB
    )
    gd0 = to_experts(sent_second)
    x1 = exchange(x0, "xlo")
    x1, g0 = lax.optimization_barrier((x1, g0))
    g1 = exchange(g0, "xlo")
    x2 = exchange(x0, "core")
    x3 = exchange(x1, "core")
    act, pre, hidden = call(
        forward,
        [wide, wide, hidden_type],
        [x0, x1, x2, x3, w_gate, w_up],
        [
            ((4, slots, quarter), BF16),
            ((4, units, quarter), BF16),
            ((4, units, quarter), BF16),
            wide,
            wide,
            hidden_type,
        ],
        15,
        8 * unit,
    )
    act, pre, hidden, gd0, g1 = lax.optimization_barrier((act, pre, hidden, gd0, g1))
    mine, theirs = call(
        hidden_grads,
        [wide, wide],
        [g0, g1, gd0, w_down, near_down],
        [((slots, half), BF16), ((2 * units, half), BF16), ((2 * units, slots), F32)],
        11,
        4 * unit,
    )
    theirs, far_both = lax.optimization_barrier((theirs, far_both))
    got = exchange(theirs, "core")
    (last_both,) = call(pass_on, [tall], [far_both], [tall], 2, 1000)
    last_both = exchange(last_both, "core")
    (own,) = call(
        cotangents,
        [pack],
        [mine, got, act, pre, hidden],
        [wide, wide, wide, wide, hidden_type, pack],
        6,
        10 * slots * units,
        8 * MIB,
    )
    far = exchange(own, "xlo")
    near = exchange(own, "core")
    total = ((slots, quarter), F32)
    (begun,) = call(
        near_row_grad,
        [total],
        [own, near, w_gate, w_up, near_both],
        [pack, pack, tall, tall, total],
        6,
        4 * unit,
    )
    far, begun, g0, g1, gd0, hidden, own = lax.optimization_barrier(
        (far, begun, g0, g1, gd0, hidden, own)
    )
    last = exchange(far, "core")
    tail = ((TAIL, slots), BF16)
    returned = ((slots, quarter + LANES), BF16)
    (sent_r,) = call(
        row_grad,
        [returned],
        [begun, own, near, far, last, far_both, last_both],
        [total, tail, tail, pack, pack, tall, tall, returned],
        9,
        4 * unit,
    )
    sent_r, own, hidden, g0, g1, gd0 = lax.optimization_barrier(
        (sent_r, own, hidden, g0, g1, gd0)
    )
    back = to_tokens(sent_r)
    g2, g3, gd1 = exchange(g0, "core"), exchange(g1, "core"), exchange(gd0, "core")
    grad_gate, grad_up = call(
        weight_grads,
        [(w_gate.shape, BF16), (w_up.shape, BF16)],
        [own, x0, x1, x2, x3],
        [((2 * units, slots), BF16), ((4, slots, quarter), BF16), ((4, 2 * units, quarter), BF16)],
        13,
        8 * unit,
    )
    (grad_down,) = call(
        weight_grads_down,
        [(w_down.shape, BF16)],
        [hidden, g0, g1, g2, g3, gd0, gd1],
        [
            hidden_type,
            ((4, slots, eighth), BF16),
            ((2, slots, quarter), BF16),
            ((4, units, eighth), BF16),
            ((2, units, quarter), BF16),
        ],
        13,
        4 * unit,
    )
    back, grad_gate, grad_up, grad_down = lax.optimization_barrier(
        (back, grad_gate, grad_up, grad_down)
    )
    input_grad, gate_grad = call(
        combine,
        [((rows, quarter), BF16), ((2, rows), F32)],
        [first, second, back, gates],
        [chosen, chosen, returned, ((2, rows), F32), ((rows, quarter), BF16), ((2, rows), F32)],
        8,
        unit,
        8 * MIB,
    )
    return input_grad, gate_grad.T, grad_gate, grad_up, grad_down


def solution(mesh):
    dp, wide, narrow = (mesh.shape[name] for name in ("dp", "wide", "narrow"))
    fine = Mesh(mesh.devices.reshape(2, dp // 2, 2, wide // 2, narrow), ALL)
    by_row, by_part = P(ROWS, None), P(ROWS, PARTS, None)
    return jax.shard_map(
        body,
        mesh=fine,
        in_specs=(by_row, by_row, by_row, by_row, by_part, by_part, by_part),
        out_specs=(P(ROWS, PARTS), by_row, by_part, by_part, by_part),
        check_vma=False,
    )
```

time: 511 us -> 173 us (0.34)
  waiting for transfers between devices: 368 us -> 84.2 us
  Pallas kernels: 0 us -> 44.6 us
  matrix products: 40.8 us -> 0 us
  other arithmetic: 16.1 us -> 0 us
  local copies, waits for them, and re-layouts: 21.4 us -> 5.34 us
  blocking collectives: 13.4 us -> 0 us
  between operations: 14.2 us -> 1.16 us
    all_to_all x4 -> x3, waiting for transfers between devices: 367 us -> 28.7 us  [the longest x1 23.4 us: to_tokens(): lax.all_to_all(shaped, ROWS, split_axis=0, concat_axis=0, tiled=True)]
    ppermute x0 -> x15, waiting for transfers between devices: none -> 55.5 us  [exchange(): return lax.ppermute(value, axis, [(0, 1), (1, 0)])]
    pallas_call x0 -> x15, Pallas kernels: none -> 44.6 us  [call(): pl.pallas_call(kernel, out_shape=[jax.ShapeDtypeStruct(s, t) for s, t in...]
    dot_general x10 -> x0, matrix products: 40.8 us -> none  [the longest x1 5.13 us: body(): jnp.einsum('rd,hd->rh', grad_rows, down_mat, preferred_element_type=jnp.f...]
    gather x4 -> x0, local copies, waits for them, and re-layouts: 17 us -> none  [the longest x2 14.9 us: body(): jnp.take(back_grad, position, axis=0).reshape(tok_rows, TOP, part_width)]
    psum x1 -> x0, blocking collectives: 13.4 us -> none  [body(): gate_grad = lax.psum(token_dots, 'dp')]
    reduce_sum x3 -> x0, other arithmetic: 11.5 us -> none  [the longest x1 11.2 us: body(): token_grad = jnp.sum(pair_rows * gates[:, :, None], axis=1)]
    all_to_all x4 -> x3, starting transfers between devices: 35.6 us -> 34.2 us  [the longest x2 24.8 us: to_experts(): lax.all_to_all(shaped, ALL, split_axis=0, concat_axis=0, tiled=True, axis...]
  transfers between devices with their start and end apart: 5 -> 18, of which waited for: 5 -> 10; matrix products, arithmetic and copies ran while one was open for 7% -> 0% of each run, Pallas kernels for 0% -> 17%
where the time goes in v2:
time: 173 us; the launch traced here: 172 us
  waiting for transfers between devices  84.2 us (49%)
  Pallas kernels  44.6 us (26%)
  starting transfers between devices  37.2 us (22%)
  local copies, waits for them, and re-layouts  5.34 us (3%)
    ppermute x15, waiting for transfers between devices, exchange(): return lax.ppermute(value, axis, [(0, 1), (1, 0)])  55.5 us
    pallas_call x15, Pallas kernels, call(): pl.pallas_call(kernel, out_shape=[jax.ShapeDtypeStruct(s, t) for s, t in...  44.6 us
    all_to_all x2, starting transfers between devices, to_experts(): lax.all_to_all(shaped, ALL, split_axis=0, concat_axis=0, tiled=True, axis...  24.8 us
    all_to_all x1, waiting for transfers between devices, to_tokens(): lax.all_to_all(shaped, ROWS, split_axis=0, concat_axis=0, tiled=True)  23.4 us
    all_to_all x1, starting transfers between devices, to_tokens(): lax.all_to_all(shaped, ROWS, split_axis=0, concat_axis=0, tiled=True)  9.36 us
    unnamed x44, local copies, waits for them, and re-layouts  5.34 us
    all_to_all x2, waiting for transfers between devices, to_experts(): lax.all_to_all(shaped, ALL, split_axis=0, concat_axis=0, tiled=True, axis...  5.3 us
  transfers between devices with their start and end apart: 18, of which 10 were waited for; matrix products, arithmetic and copies ran while one was open for 0% of the time, Pallas kernels for 17%

profile of v2, /device:TPU:24, one launch (start us, length us, event | category | flops | bytes accessed | tf_op | source)
XLA Modules:
  0.0 172.5 jit_solution(9581925455906818916)
XLA Ops:
  0.6 2.5 %shard_map.110 = bf16[512,1536]{1,0:T(8,128)(2,1)} custom-call(s32[2,128]{1,0:T(2,128)} %bitcast.18, bf16[128,4096]{1,0:T(8,128)(2,1)} %x_hbm.1, bf16[128,4096]{1,0:T(8,128)(2,1)} %g_hbm.3), custom_call_target="tpu_custom_call" | custom-call | flops 100663296 | bytes 3671040 | tf_op jit(solution)/shard_map/pallas_call | solution.py:60
  3.2 14.1 %all-to-all-start = ((bf16[64,8,1536]{2,1,0:T(8,128)(2,1)}), bf16[64,8,1536]{2,1,0:T(8,128)(2,1)S(1)}, u32[]{:S(2)}, u32[]{:S(2)}) async-start(bf16[64,8,1536]{2,1,0:T(8,128)(2,1)} %bitcast.15), calls=%async_computation | async-start | bytes 3145728 | tf_op jit(solution)/shard_map/all_to_all | solution.py:445
  17.2 2.3 %shard_map.114 = bf16[384,2048]{1,0:T(8,128)(2,1)} custom-call(bf16[1,192,4096]{2,1,0:T(8,128)(2,1)} %gate_hbm.7, bf16[1,192,4096]{2,1,0:T(8,128)(2,1)} %up_hbm.7), custom_call_target="tpu_custom_call" | custom-call | flops 1000 | bytes 4718592 | tf_op jit(solution)/shard_map/pallas_call | solution.py:60
  19.6 0.3 collective-permute-start.2
  19.9 2.5 %shard_map.113 = (bf16[384,1024]{1,0:T(8,128)(2,1)}, bf16[192,2048]{1,0:T(8,128)(2,1)}) custom-call(bf16[1,192,4096]{2,1,0:T(8,128)(2,1)} %gate_hbm.7, bf16[1,192,4096]{2,1,0:T(8,128)(2,1)} %up_hbm.7, bf16[1,192,4096]{2,1,0:T(8,128)(2,1)} %down_hbm.3), custom_call_target="tpu_custom_call" | custom-call | flops 1000 | bytes 6291456 | tf_op jit(solution)/shard_map/pallas_call | solution.py:60
  22.4 0.1 collective-permute-start
  22.5 0.5 collective-permute-start.1
  23.0 1.7 shard_map.112
  24.7 2.3 %shard_map.111 = bf16[512,1024]{1,0:T(8,128)(2,1)} custom-call(s32[2,128]{1,0:T(2,128)} %bitcast.20, bf16[128,4096]{1,0:T(8,128)(2,1)} %g_hbm.3), custom_call_target="tpu_custom_call" | custom-call | flops 100663296 | bytes 2098176 | tf_op jit(solution)/shard_map/pallas_call | solution.py:60
  27.0 28.4 %collective-permute-done.2.both_hbm.far_both = bf16[384,2048]{1,0:T(8,128)(2,1)S(1)} collective-permute-done((bf16[384,2048]{1,0:T(8,128)(2,1)}, bf16[384,2048]{1,0:T(8,128)(2,1)S(1)}, u32[]{:S(2)}, u32[]{:S(2)}) %collective-permute-start.2) | collective-permute-done | bytes 1572896 | tf_op jit(solution)/shard_map/ppermute | solution.py:441
  55.4 3.2 %all-to-all-done = bf16[64,8,1536]{2,1,0:T(8,128)(2,1)S(1)} async-done(((bf16[64,8,1536]{2,1,0:T(8,128)(2,1)}), bf16[64,8,1536]{2,1,0:T(8,128)(2,1)S(1)}, u32[]{:S(2)}, u32[]{:S(2)}) %all-to-all-start) | async-done | bytes 1572896 | tf_op jit(solution)/shard_map/all_to_all | solution.py:445
  58.6 1.0 shard_map.115
  59.6 0.0 copy-start.3
  59.7 0.1 collective-permute-start.3
  59.8 10.7 %all-to-all-start.1 = ((bf16[64,8,1024]{2,1,0:T(8,128)(2,1)}), bf16[64,8,1024]{2,1,0:T(8,128)(2,1)S(1)}, u32[]{:S(2)}, u32[]{:S(2)}) async-start(bf16[64,8,1024]{2,1,0:T(8,128)(2,1)} %bitcast.17), calls=%async_computation.1 | async-start | bytes 2097152 | tf_op jit(solution)/shard_map/all_to_all | solution.py:445
  70.5 0.1 collective-permute-start.4
  70.6 12.1 %collective-permute-done.3.x1 = bf16[512,1024]{1,0:T(8,128)(2,1)} collective-permute-done((bf16[512,1024]{1,0:T(8,128)(2,1)S(1)}, bf16[512,1024]{1,0:T(8,128)(2,1)}, u32[]{:S(2)}, u32[]{:S(2)}) %collective-permute-start.3) | collective-permute-done | bytes 1048608 | tf_op jit(solution)/shard_map/ppermute | solution.py:441
  82.7 0.3 collective-permute-start.6
  83.0 1.0 copy-done.17
  84.0 1.7 collective-permute-done.5.x3
  85.7 5.9 %shard_map.116 = (f32[192,512]{1,0:T(8,128)}, f32[192,512]{1,0:T(8,128)}, bf16[192,512]{1,0:T(8,128)(2,1)}) custom-call(bf16[512,1024]{1,0:T(8,128)(2,1)} %copy-done.3, bf16[512,1024]{1,0:T(8,128)(2,1)} %collective-permute-done.3.x1, bf16[512,1024]{1,0:T(8,128)(2,1)} %copy-done.17, bf16[512,1024]{1,0:T(8,128)(2,1)} %collective-permute-done.5.x3, ...), custom_call_target="tpu_custom_call" | custom-call | flops 1610612736 | bytes 8323072 | tf_op jit(solution)/shard_map/pallas_call | solution.py:60
  91.6 5.4 %collective-permute-done.6.g1 = bf16[512,512]{1,0:T(8,128)(2,1)S(1)} collective-permute-done((bf16[512,512]{1,0:T(8,128)(2,1)S(1)}, bf16[512,512]{1,0:T(8,128)(2,1)S(1)}, u32[]{:S(2)}, u32[]{:S(2)}) %collective-permute-start.6) | collective-permute-done | bytes 524320 | tf_op jit(solution)/shard_map/ppermute | solution.py:441
  97.0 2.1 %all-to-all-done.1 = bf16[64,8,1024]{2,1,0:T(8,128)(2,1)S(1)} async-done(((bf16[64,8,1024]{2,1,0:T(8,128)(2,1)}), bf16[64,8,1024]{2,1,0:T(8,128)(2,1)S(1)}, u32[]{:S(2)}, u32[]{:S(2)}) %all-to-all-start.1) | async-done | bytes 1048608 | tf_op jit(solution)/shard_map/all_to_all | solution.py:445
  99.2 1.0 copy-done.11
  100.1 3.6 %shard_map.117 = (f32[192,512]{1,0:T(8,128)}, f32[192,512]{1,0:T(8,128)}) custom-call(bf16[512,512]{1,0:T(8,128)(2,1)} %copy-done.1, bf16[512,512]{1,0:T(8,128)(2,1)} %copy-done.14, bf16[512,1024]{1,0:T(8,128)(2,1)} %bitcast.12, bf16[1,192,4096]{2,1,0:T(8,128)(2,1)} %down_hbm.3, bf16[192,2048]{1,0:T(8,128)(2,1)} %collective-permute-done.1.near_hbm), custom_call_target="tpu_custom_call" | custom-call | flops 805306368 | bytes 5242880 | tf_op jit(solution)/shard_map/pallas_call | solution.py:60
  103.8 0.1 collective-permute-start.7
  103.9 1.9 %collective-permute-done.7.got_hbm = f32[192,512]{1,0:T(8,128)S(1)} collective-permute-done((f32[192,512]{1,0:T(8,128)}, f32[192,512]{1,0:T(8,128)S(1)}, u32[]{:S(2)}, u32[]{:S(2)}) %collective-permute-start.7) | collective-permute-done | bytes 393248 | tf_op jit(solution)/shard_map/ppermute | solution.py:441
  105.8 0.0 copy-start.7
  105.8 1.0 copy-done.7
  106.8 1.4 shard_map.118.own_hbm.pack_hbm
  108.2 0.4 collective-permute-start.9
  108.6 2.0 %shard_map.120 = bf16[384,1024]{1,0:T(8,128)(2,1)} custom-call(bf16[384,2048]{1,0:T(8,128)(2,1)} %copy-done.13), custom_call_target="tpu_custom_call" | custom-call | flops 1000 | bytes 2359296 | tf_op jit(solution)/shard_map/pallas_call | solution.py:60
  110.7 0.5 collective-permute-start.11
  111.1 0.8 copy-done.16
  111.9 4.3 %shard_map.119.begun_hbm = f32[512,1024]{1,0:T(8,128)} custom-call(bf16[400,512]{1,0:T(8,128)(2,1)} %copy-done, bf16[400,512]{1,0:T(8,128)(2,1)} %copy-done.16, bf16[1,192,4096]{2,1,0:T(8,128)(2,1)} %gate_hbm.7, bf16[1,192,4096]{2,1,0:T(8,128)(2,1)} %up_hbm.7, bf16[384,1024]{1,0:T(8,128)(2,1)} %collective-permute-done.both_hbm), custom_call_target="tpu_custom_call" | custom-call | flops 805306368 | bytes 6848512 | tf_op jit(solution)/shard_map/pallas_call | solution.py:60
  116.2 4.2 %collective-permute-done.8.far_hbm = bf16[400,512]{1,0:T(8,128)(2,1)S(1)} collective-permute-done((bf16[400,512]{1,0:T(8,128)(2,1)S(1)}, bf16[400,512]{1,0:T(8,128)(2,1)S(1)}, u32[]{:S(2)}, u32[]{:S(2)}) %collective-permute-start.8) | collective-permute-done | bytes 409632 | tf_op jit(solution)/shard_map/ppermute | solution.py:441
  120.4 1.7 %collective-permute-done.10.last_hbm = bf16[400,512]{1,0:T(8,128)(2,1)S(1)} collective-permute-done((bf16[400,512]{1,0:T(8,128)(2,1)S(1)}, bf16[400,512]{1,0:T(8,128)(2,1)S(1)}, u32[]{:S(2)}, u32[]{:S(2)}) %collective-permute-start.10) | collective-permute-done | bytes 409632 | tf_op jit(solution)/shard_map/ppermute | solution.py:441
  122.1 0.8 copy-done.21
  122.9 4.5 %shard_map.121 = bf16[512,1152]{1,0:T(8,128)(2,1)} custom-call(f32[512,1024]{1,0:T(8,128)} %shard_map.119.begun_hbm, bf16[400,512]{1,0:T(8,128)(2,1)} %copy-done, bf16[400,512]{1,0:T(8,128)(2,1)} %copy-done.16, bf16[400,512]{1,0:T(8,128)(2,1)} %copy-done.20, bf16[400,512]{1,0:T(8,128)(2,1)} %copy-done.21, bf16[384,2048]{1,0:T(8,128)(2,1)} %copy-done.13, ...), custom_call_target="tpu_custom_call" | custom-call | flops 805306368 | bytes 7274496 | tf_op jit(solution)/shard_map/pallas_call | solution.py:60
  127.5 9.4 %all-to-all-start.2 = ((bf16[64,8,1152]{2,1,0:T(8,128)(2,1)}), bf16[64,8,1152]{2,1,0:T(8,128)(2,1)S(1)}, u32[]{:S(2)}, u32[]{:S(2)}) async-start(bf16[64,8,1152]{2,1,0:T(8,128)(2,1)} %bitcast.16), calls=%async_computation.2 | async-start | bytes 2359296 | tf_op jit(solution)/shard_map/all_to_all | solution.py:452
  136.8 0.1 collective-permute-start.14
  136.9 0.5 collective-permute-start.12
  137.4 0.1 collective-permute-start.13
  137.5 4.6 %shard_map.122 = (bf16[1,192,4096]{2,1,0:T(8,128)(2,1)}, bf16[1,192,4096]{2,1,0:T(8,128)(2,1)}) custom-call(bf16[400,512]{1,0:T(8,128)(2,1)} %copy-done, bf16[512,1024]{1,0:T(8,128)(2,1)} %copy-done.3, bf16[512,1024]{1,0:T(8,128)(2,1)} %collective-permute-done.3.x1, bf16[512,1024]{1,0:T(8,128)(2,1)} %copy-done.17, bf16[512,1024]{1,0:T(8,128)(2,1)} %collective-permute-done.5.x3), custom_call_target="tpu_custom_call" | custom-call | flops 1610612736 | bytes 7749632 | tf_op jit(solution)/shard_map/pallas_call | solution.py:60
  142.3 0.8 copy-done.19
  143.1 3.9 %shard_map.123 = bf16[1,192,4096]{2,1,0:T(8,128)(2,1)} custom-call(bf16[192,512]{1,0:T(8,128)(2,1)} %get-tuple-element.91.hidden_hbm, bf16[512,512]{1,0:T(8,128)(2,1)} %copy-done.1, bf16[512,512]{1,0:T(8,128)(2,1)} %copy-done.14, bf16[512,512]{1,0:T(8,128)(2,1)} %copy-done.19, bf16[512,512]{1,0:T(8,128)(2,1)} %collective-permute-done.13.g3, ...), custom_call_target="tpu_custom_call" | custom-call | flops 805306368 | bytes 5963776 | tf_op jit(solution)/shard_map/pallas_call | solution.py:60
  146.9 23.4 %all-to-all-done.2 = bf16[64,8,1152]{2,1,0:T(8,128)(2,1)S(1)} async-done(((bf16[64,8,1152]{2,1,0:T(8,128)(2,1)}), bf16[64,8,1152]{2,1,0:T(8,128)(2,1)S(1)}, u32[]{:S(2)}, u32[]{:S(2)}) %all-to-all-start.2) | async-done | bytes 1179680 | tf_op jit(solution)/shard_map/all_to_all | solution.py:452
  170.4 1.9 %shard_map.124 = (bf16[128,1024]{1,0:T(8,128)(2,1)}, f32[2,128]{1,0:T(2,128)}) custom-call(bf16[128,512]{1,0:T(8,128)(2,1)S(1)} %copy-done.8, bf16[128,512]{1,0:T(8,128)(2,1)S(1)} %copy-done.9, bf16[512,1152]{1,0:T(8,128)(2,1)S(1)} %bitcast.10, f32[2,128]{1,0:T(2,128)S(1)} %bitcast.11), custom_call_target="tpu_custom_call" | custom-call | flops 201326592 | bytes 1705984 | tf_op jit(solution)/shard_map/pallas_call | solution.py:60
  (47 shorter events, 0.1 us)
Async XLA Ops:
  3.2 55.4 %all-to-all-start = ((bf16[64,8,1536]{2,1,0:T(8,128)(2,1)}), bf16[64,8,1536]{2,1,0:T(8,128)(2,1)S(1)}, u32[]{:S(2)}, u32[]{:S(2)}) async-start(bf16[64,8,1536]{2,1,0:T(8,128)(2,1)} %bitcast.15), calls=%async_computation | async-start | bytes 3145728 | tf_op jit(solution)/shard_map/all_to_all | solution.py:445
  19.6 35.9 %collective-permute-start.2 = (bf16[384,2048]{1,0:T(8,128)(2,1)}, bf16[384,2048]{1,0:T(8,128)(2,1)S(1)}, u32[]{:S(2)}, u32[]{:S(2)}) collective-permute-start(bf16[384,2048]{1,0:T(8,128)(2,1)} %shard_map.114), channel_id=1, source_target_pairs={{0,128},{128,0},{1,129},{129,1},{2,130},{130,2},{3,131},{131,3},{4... | collective-permute-start | bytes 4718600 | tf_op jit(solution)/shard_map/ppermute | solution.py:441
  22.4 4.6 %collective-permute-start = (bf16[384,1024]{1,0:T(8,128)(2,1)}, bf16[384,1024]{1,0:T(8,128)(2,1)}, u32[]{:S(2)}, u32[]{:S(2)}) collective-permute-start(bf16[384,1024]{1,0:T(8,128)(2,1)} %get-tuple-element.55), channel_id=1, source_target_pairs={{0,64},{64,0},{1,65},{65,1},{2,66},{66,2},{3,67},{67,3},{4,68},{68... | collective-permute-start | bytes 2359304 | tf_op jit(solution)/shard_map/ppermute | solution.py:441
  22.5 4.5 %collective-permute-start.1 = (bf16[192,2048]{1,0:T(8,128)(2,1)}, bf16[192,2048]{1,0:T(8,128)(2,1)}, u32[]{:S(2)}, u32[]{:S(2)}) collective-permute-start(bf16[192,2048]{1,0:T(8,128)(2,1)} %get-tuple-element.56), channel_id=1, source_target_pairs={{0,64},{64,0},{1,65},{65,1},{2,66},{66,2},{3,67},{67,3},{4,68},{68... | collective-permute-start | bytes 2359304 | tf_op jit(solution)/shard_map/ppermute | solution.py:441
  55.4 3.2 %copy-start.13 = (bf16[384,2048]{1,0:T(8,128)(2,1)}, bf16[384,2048]{1,0:T(8,128)(2,1)S(1)}, u32[]{:S(2)}) copy-start(bf16[384,2048]{1,0:T(8,128)(2,1)S(1)} %collective-permute-done.2.both_hbm.far_both) | copy-start | bytes 4718596
  59.6 26.1 %copy-start.3 = (bf16[512,1024]{1,0:T(8,128)(2,1)}, bf16[512,1024]{1,0:T(8,128)(2,1)S(1)}, u32[]{:S(2)}) copy-start(bf16[512,1024]{1,0:T(8,128)(2,1)S(1)} %get-tuple-element.60.x0) | copy-start | bytes 3145732
  59.6 32.0 %copy-start.1 = (bf16[512,512]{1,0:T(8,128)(2,1)}, bf16[512,512]{1,0:T(8,128)(2,1)S(1)}, u32[]{:S(2)}) copy-start(bf16[512,512]{1,0:T(8,128)(2,1)S(1)} %get-tuple-element.92.g0) | copy-start | bytes 1572868
  59.7 23.0 %collective-permute-start.3 = (bf16[512,1024]{1,0:T(8,128)(2,1)S(1)}, bf16[512,1024]{1,0:T(8,128)(2,1)}, u32[]{:S(2)}, u32[]{:S(2)}) collective-permute-start(bf16[512,1024]{1,0:T(8,128)(2,1)S(1)} %get-tuple-element.60.x0), channel_id=1, source_target_pairs={{0,128},{128,0},{1,129},{129,1},{2,130},{130,2},{3,131},{131,3},{4... | collective-permute-start | bytes 3145736 | tf_op jit(solution)/shard_map/ppermute | solution.py:441
  59.8 39.4 %all-to-all-start.1 = ((bf16[64,8,1024]{2,1,0:T(8,128)(2,1)}), bf16[64,8,1024]{2,1,0:T(8,128)(2,1)S(1)}, u32[]{:S(2)}, u32[]{:S(2)}) async-start(bf16[64,8,1024]{2,1,0:T(8,128)(2,1)} %bitcast.17), calls=%async_computation.1 | async-start | bytes 2097152 | tf_op jit(solution)/shard_map/all_to_all | solution.py:445
  70.5 12.5 %collective-permute-start.4 = (bf16[512,1024]{1,0:T(8,128)(2,1)S(1)}, bf16[512,1024]{1,0:T(8,128)(2,1)S(1)}, u32[]{:S(2)}, u32[]{:S(2)}) collective-permute-start(bf16[512,1024]{1,0:T(8,128)(2,1)S(1)} %get-tuple-element.60.x0), channel_id=1, source_target_pairs={{0,64},{64,0},{1,65},{65,1},{2,66},{66,2},{3,67},{67,3},{4,68},{68... | collective-permute-start | bytes 3145736 | tf_op jit(solution)/shard_map/ppermute | solution.py:441
  82.7 3.0 %collective-permute-start.5 = (bf16[512,1024]{1,0:T(8,128)(2,1)}, bf16[512,1024]{1,0:T(8,128)(2,1)}, u32[]{:S(2)}, u32[]{:S(2)}) collective-permute-start(bf16[512,1024]{1,0:T(8,128)(2,1)} %collective-permute-done.3.x1), channel_id=1, source_target_pairs={{0,64},{64,0},{1,65},{65,1},{2,66},{66,2},{3,67},{67,3},{4,68},{68... | collective-permute-start | bytes 3145736 | tf_op jit(solution)/shard_map/ppermute | solution.py:441
  82.7 14.3 %collective-permute-start.6 = (bf16[512,512]{1,0:T(8,128)(2,1)S(1)}, bf16[512,512]{1,0:T(8,128)(2,1)S(1)}, u32[]{:S(2)}, u32[]{:S(2)}) collective-permute-start(bf16[512,512]{1,0:T(8,128)(2,1)S(1)} %get-tuple-element.92.g0), channel_id=1, source_target_pairs={{0,128},{128,0},{1,129},{129,1},{2,130},{130,2},{3,131},{131,3},{4... | collective-permute-start | bytes 1572872 | tf_op jit(solution)/shard_map/ppermute | solution.py:441
  83.0 1.0 copy-start.17
  97.0 2.1 %copy-start.14 = (bf16[512,512]{1,0:T(8,128)(2,1)}, bf16[512,512]{1,0:T(8,128)(2,1)S(1)}, u32[]{:S(2)}) copy-start(bf16[512,512]{1,0:T(8,128)(2,1)S(1)} %collective-permute-done.6.g1) | copy-start | bytes 1572868
  99.2 1.0 copy-start.11
  100.1 5.7 %copy-start.4 = (bf16[192,512]{1,0:T(8,128)(2,1)S(1)}, bf16[192,512]{1,0:T(8,128)(2,1)}, u32[]{:S(2)}) copy-start(bf16[192,512]{1,0:T(8,128)(2,1)} %get-tuple-element.91.hidden_hbm) | copy-start | bytes 589828
  100.1 5.7 %copy-start.5 = (f32[192,512]{1,0:T(8,128)S(1)}, f32[192,512]{1,0:T(8,128)}, u32[]{:S(2)}) copy-start(f32[192,512]{1,0:T(8,128)} %get-tuple-element.75.act_hbm) | copy-start | bytes 1179652
  100.1 5.7 %copy-start.6 = (f32[192,512]{1,0:T(8,128)S(1)}, f32[192,512]{1,0:T(8,128)}, u32[]{:S(2)}) copy-start(f32[192,512]{1,0:T(8,128)} %get-tuple-element.76.pre_hbm) | copy-start | bytes 1179652
  103.8 2.0 %collective-permute-start.7 = (f32[192,512]{1,0:T(8,128)}, f32[192,512]{1,0:T(8,128)S(1)}, u32[]{:S(2)}, u32[]{:S(2)}) collective-permute-start(f32[192,512]{1,0:T(8,128)} %get-tuple-element.74), channel_id=1, source_target_pairs={{0,64},{64,0},{1,65},{65,1},{2,66},{66,2},{3,67},{67,3},{4,68},{68... | collective-permute-start | bytes 1179656 | tf_op jit(solution)/shard_map/ppermute | solution.py:441
  105.8 1.0 copy-start.7
  108.2 2.9 %copy-start = (bf16[400,512]{1,0:T(8,128)(2,1)}, bf16[400,512]{1,0:T(8,128)(2,1)S(1)}, u32[]{:S(2)}) copy-start(bf16[400,512]{1,0:T(8,128)(2,1)S(1)} %shard_map.118.own_hbm.pack_hbm) | copy-start | bytes 1228804
  108.2 2.9 %collective-permute-start.9 = (bf16[400,512]{1,0:T(8,128)(2,1)S(1)}, bf16[400,512]{1,0:T(8,128)(2,1)S(1)}, u32[]{:S(2)}, u32[]{:S(2)}) collective-permute-start(bf16[400,512]{1,0:T(8,128)(2,1)S(1)} %shard_map.118.own_hbm.pack_hbm), channel_id=1, source_target_pairs={{0,64},{64,0},{1,65},{65,1},{2,66},{66,2},{3,67},{67,3},{4,68},{68... | collective-permute-start | bytes 1228808 | tf_op jit(solution)/shard_map/ppermute | solution.py:441
  108.6 11.7 %collective-permute-start.8 = (bf16[400,512]{1,0:T(8,128)(2,1)S(1)}, bf16[400,512]{1,0:T(8,128)(2,1)S(1)}, u32[]{:S(2)}, u32[]{:S(2)}) collective-permute-start(bf16[400,512]{1,0:T(8,128)(2,1)S(1)} %shard_map.118.own_hbm.pack_hbm), channel_id=1, source_target_pairs={{0,128},{128,0},{1,129},{129,1},{2,130},{130,2},{3,131},{131,3},{4... | collective-permute-start | bytes 1228808 | tf_op jit(solution)/shard_map/ppermute | solution.py:441
  110.7 9.7 %collective-permute-start.11 = (bf16[384,1024]{1,0:T(8,128)(2,1)}, bf16[384,1024]{1,0:T(8,128)(2,1)S(1)}, u32[]{:S(2)}, u32[]{:S(2)}) collective-permute-start(bf16[384,1024]{1,0:T(8,128)(2,1)} %shard_map.120), channel_id=1, source_target_pairs={{0,64},{64,0},{1,65},{65,1},{2,66},{66,2},{3,67},{67,3},{4,68},{68... | collective-permute-start | bytes 2359304 | tf_op jit(solution)/shard_map/ppermute | solution.py:441
  111.1 0.8 copy-start.16
  120.4 1.8 %copy-start.20 = (bf16[400,512]{1,0:T(8,128)(2,1)}, bf16[400,512]{1,0:T(8,128)(2,1)S(1)}, u32[]{:S(2)}) copy-start(bf16[400,512]{1,0:T(8,128)(2,1)S(1)} %collective-permute-done.8.far_hbm) | copy-start | bytes 1228804
  120.4 1.7 %collective-permute-start.10 = (bf16[400,512]{1,0:T(8,128)(2,1)S(1)}, bf16[400,512]{1,0:T(8,128)(2,1)S(1)}, u32[]{:S(2)}, u32[]{:S(2)}) collective-permute-start(bf16[400,512]{1,0:T(8,128)(2,1)S(1)} %collective-permute-done.8.far_hbm), channel_id=1, source_target_pairs={{0,64},{64,0},{1,65},{65,1},{2,66},{66,2},{3,67},{67,3},{4,68},{68... | collective-permute-start | bytes 1228808 | tf_op jit(solution)/shard_map/ppermute | solution.py:441
  120.4 1.7 %copy-start.18 = (bf16[384,1024]{1,0:T(8,128)(2,1)}, bf16[384,1024]{1,0:T(8,128)(2,1)S(1)}, u32[]{:S(2)}) copy-start(bf16[384,1024]{1,0:T(8,128)(2,1)S(1)} %collective-permute-done.11.last_both) | copy-start | bytes 2359300
  122.1 0.8 copy-start.21
  127.4 9.4 %copy-start.12 = (bf16[64,8,1024]{2,1,0:T(8,128)(2,1)S(1)}, bf16[64,8,1024]{2,1,0:T(8,128)(2,1)}, u32[]{:S(2)}) copy-start(bf16[64,8,1024]{2,1,0:T(8,128)(2,1)} %copy-done.11) | copy-start | bytes 3145732
  127.4 9.5 %copy-start.2 = (bf16[512,512]{1,0:T(8,128)(2,1)S(1)}, bf16[512,512]{1,0:T(8,128)(2,1)}, u32[]{:S(2)}) copy-start(bf16[512,512]{1,0:T(8,128)(2,1)} %copy-done.1) | copy-start | bytes 1572868
  127.4 10.0 %copy-start.15 = (bf16[512,512]{1,0:T(8,128)(2,1)S(1)}, bf16[512,512]{1,0:T(8,128)(2,1)}, u32[]{:S(2)}) copy-start(bf16[512,512]{1,0:T(8,128)(2,1)} %copy-done.14) | copy-start | bytes 1572868
  127.5 42.9 %all-to-all-start.2 = ((bf16[64,8,1152]{2,1,0:T(8,128)(2,1)}), bf16[64,8,1152]{2,1,0:T(8,128)(2,1)S(1)}, u32[]{:S(2)}, u32[]{:S(2)}) async-start(bf16[64,8,1152]{2,1,0:T(8,128)(2,1)} %bitcast.16), calls=%async_computation.2 | async-start | bytes 2359296 | tf_op jit(solution)/shard_map/all_to_all | solution.py:452
  136.8 5.4 %collective-permute-start.14 = (bf16[512,1024]{1,0:T(8,128)(2,1)S(1)}, bf16[512,1024]{1,0:T(8,128)(2,1)}, u32[]{:S(2)}, u32[]{:S(2)}) collective-permute-start(bf16[512,1024]{1,0:T(8,128)(2,1)S(1)} %bitcast.14), channel_id=1, source_target_pairs={{0,64},{64,0},{1,65},{65,1},{2,66},{66,2},{3,67},{67,3},{4,68},{68... | collective-permute-start | bytes 3145736 | tf_op jit(solution)/shard_map/ppermute | solution.py:441
  136.9 5.3 %collective-permute-start.12 = (bf16[512,512]{1,0:T(8,128)(2,1)S(1)}, bf16[512,512]{1,0:T(8,128)(2,1)S(1)}, u32[]{:S(2)}, u32[]{:S(2)}) collective-permute-start(bf16[512,512]{1,0:T(8,128)(2,1)S(1)} %copy-done.2), channel_id=1, source_target_pairs={{0,64},{64,0},{1,65},{65,1},{2,66},{66,2},{3,67},{67,3},{4,68},{68... | collective-permute-start | bytes 1572872 | tf_op jit(solution)/shard_map/ppermute | solution.py:441
  137.4 4.8 %collective-permute-start.13 = (bf16[512,512]{1,0:T(8,128)(2,1)S(1)}, bf16[512,512]{1,0:T(8,128)(2,1)}, u32[]{:S(2)}, u32[]{:S(2)}) collective-permute-start(bf16[512,512]{1,0:T(8,128)(2,1)S(1)} %copy-done.15), channel_id=1, source_target_pairs={{0,64},{64,0},{1,65},{65,1},{2,66},{66,2},{3,67},{67,3},{4,68},{68... | collective-permute-start | bytes 1572872 | tf_op jit(solution)/shard_map/ppermute | solution.py:441
  142.2 28.1 %copy-start.8 = (bf16[128,512]{1,0:T(8,128)(2,1)S(1)}, bf16[128,512]{1,0:T(8,128)(2,1)}, u32[]{:S(2)}) copy-start(bf16[128,512]{1,0:T(8,128)(2,1)} %get-tuple-element.57.first_hbm) | copy-start | bytes 393220
  142.2 28.1 %copy-start.9 = (bf16[128,512]{1,0:T(8,128)(2,1)S(1)}, bf16[128,512]{1,0:T(8,128)(2,1)}, u32[]{:S(2)}) copy-start(bf16[128,512]{1,0:T(8,128)(2,1)} %get-tuple-element.58.second_hbm) | copy-start | bytes 393220
  142.2 28.1 %copy-start.10 = (f32[128,2]{0,1:T(2,128)S(1)}, f32[128,2]{0,1:T(2,128)}, u32[]{:S(2)}) copy-start(f32[128,2]{0,1:T(2,128)} %param.10) | copy-start | bytes 3076
  142.2 0.8 copy-start.19

commit v3 on v2

--- a/solution.py
+++ b/solution.py
@@ -491,10 +491,8 @@
         unit // 2,
     )
     first, second = call(pick, [chosen, chosen], [ids], [id_type, chosen, chosen], 3, unit // 4)
-    got_first, sent_second, first, second, near_both, near_down, far_both = (
-        lax.optimization_barrier(
-            (got_first, sent_second, first, second, near_both, near_down, far_both)
-        )
+    got_first, first, second, near_both, near_down, far_both = lax.optimization_barrier(
+        (got_first, first, second, near_both, near_down, far_both)
     )
     eighth_piece = ((slots, eighth), BF16)
     x0, g0 = call(
@@ -520,6 +518,7 @@
         ],
         15,
         8 * unit,
+        63 * MIB,
     )
     act, pre, hidden, gd0, g1 = lax.optimization_barrier((act, pre, hidden, gd0, g1))
     mine, theirs = call(

time: 173 us -> 172 us (level)
  starting transfers between devices: 37.2 us -> 35 us
    all_to_all x2, waiting for transfers between devices: 5.3 us -> 13.2 us  [to_experts(): lax.all_to_all(shaped, ALL, split_axis=0, concat_axis=0, tiled=True, axis...]
    ppermute x15, waiting for transfers between devices: 55.5 us -> 49.1 us  [exchange(): return lax.ppermute(value, axis, [(0, 1), (1, 0)])]
    all_to_all x1, starting transfers between devices: 9.36 us -> 6.92 us  [to_tokens(): lax.all_to_all(shaped, ROWS, split_axis=0, concat_axis=0, tiled=True)]
    unnamed x44 -> x40, local copies, waits for them, and re-layouts: 5.34 us -> 6.12 us
  transfers between devices with their start and end apart: 18 -> 18, of which waited for: 10 -> 11; matrix products, arithmetic and copies ran while one was open for 0% -> 0% of each run, Pallas kernels for 17% -> 17%
where the time goes in v3:
time: 172 us
  waiting for transfers between devices  84.5 us (49%)
  Pallas kernels  44.9 us (26%)
  starting transfers between devices  35 us (20%)
  local copies, waits for them, and re-layouts  6.12 us (4%)
    ppermute x15, waiting for transfers between devices, exchange(): return lax.ppermute(value, axis, [(0, 1), (1, 0)])  49.1 us
    pallas_call x15, Pallas kernels, call(): pl.pallas_call(kernel, out_shape=[jax.ShapeDtypeStruct(s, t) for s, t in...  44.9 us
    all_to_all x2, starting transfers between devices, to_experts(): lax.all_to_all(shaped, ALL, split_axis=0, concat_axis=0, tiled=True, axis...  24.9 us
    all_to_all x1, waiting for transfers between devices, to_tokens(): lax.all_to_all(shaped, ROWS, split_axis=0, concat_axis=0, tiled=True)  22.3 us
    all_to_all x2, waiting for transfers between devices, to_experts(): lax.all_to_all(shaped, ALL, split_axis=0, concat_axis=0, tiled=True, axis...  13.2 us
    all_to_all x1, starting transfers between devices, to_tokens(): lax.all_to_all(shaped, ROWS, split_axis=0, concat_axis=0, tiled=True)  6.92 us
    unnamed x40, local copies, waits for them, and re-layouts  6.12 us
  transfers between devices with their start and end apart: 18, of which 11 were waited for; matrix products, arithmetic and copies ran while one was open for 0% of the time, Pallas kernels for 17%

profile of v3, /device:TPU:24, one launch (start us, length us, event | category | flops | bytes accessed | tf_op | source)
XLA Modules:
  0.0 171.6 jit_solution(17469624600266493124)
XLA Ops:
  0.6 2.5 %shard_map.110 = bf16[512,1536]{1,0:T(8,128)(2,1)} custom-call(s32[2,128]{1,0:T(2,128)} %bitcast.15, bf16[128,4096]{1,0:T(8,128)(2,1)} %x_hbm.1, bf16[128,4096]{1,0:T(8,128)(2,1)} %g_hbm.3), custom_call_target="tpu_custom_call" | custom-call | flops 100663296 | bytes 3671040 | tf_op jit(solution)/shard_map/pallas_call | solution.py:60
  3.2 14.1 %all-to-all-start = ((bf16[64,8,1536]{2,1,0:T(8,128)(2,1)}), bf16[64,8,1536]{2,1,0:T(8,128)(2,1)S(1)}, u32[]{:S(2)}, u32[]{:S(2)}) async-start(bf16[64,8,1536]{2,1,0:T(8,128)(2,1)} %bitcast.12), calls=%async_computation | async-start | bytes 3145728 | tf_op jit(solution)/shard_map/all_to_all | solution.py:445
  17.2 2.3 %shard_map.113 = bf16[384,2048]{1,0:T(8,128)(2,1)} custom-call(bf16[1,192,4096]{2,1,0:T(8,128)(2,1)} %gate_hbm.7, bf16[1,192,4096]{2,1,0:T(8,128)(2,1)} %up_hbm.7), custom_call_target="tpu_custom_call" | custom-call | flops 1000 | bytes 4718592 | tf_op jit(solution)/shard_map/pallas_call | solution.py:60
  19.6 0.3 collective-permute-start.2
  19.9 2.6 %shard_map.112 = (bf16[384,1024]{1,0:T(8,128)(2,1)}, bf16[192,2048]{1,0:T(8,128)(2,1)}) custom-call(bf16[1,192,4096]{2,1,0:T(8,128)(2,1)} %gate_hbm.7, bf16[1,192,4096]{2,1,0:T(8,128)(2,1)} %up_hbm.7, bf16[1,192,4096]{2,1,0:T(8,128)(2,1)} %down_hbm.3), custom_call_target="tpu_custom_call" | custom-call | flops 1000 | bytes 6291456 | tf_op jit(solution)/shard_map/pallas_call | solution.py:60
  22.4 0.1 collective-permute-start
  22.6 0.5 collective-permute-start.1
  23.0 1.7 %shard_map.111 = (bf16[128,512]{1,0:T(8,128)(2,1)}, bf16[128,512]{1,0:T(8,128)(2,1)}) custom-call(s32[2,128]{1,0:T(2,128)} %bitcast.16), custom_call_target="tpu_custom_call" | custom-call | flops 50331648 | bytes 263168 | tf_op jit(solution)/shard_map/pallas_call | solution.py:60
  24.8 0.4 collective-permute-done.both_hbm
  25.2 1.1 collective-permute-done.1.near_hbm
  26.3 29.1 %collective-permute-done.2.both_hbm.far_both = bf16[384,2048]{1,0:T(8,128)(2,1)S(1)} collective-permute-done((bf16[384,2048]{1,0:T(8,128)(2,1)}, bf16[384,2048]{1,0:T(8,128)(2,1)S(1)}, u32[]{:S(2)}, u32[]{:S(2)}) %collective-permute-start.2) | collective-permute-done | bytes 1572896 | tf_op jit(solution)/shard_map/ppermute | solution.py:441
  55.4 3.2 %all-to-all-done = bf16[64,8,1536]{2,1,0:T(8,128)(2,1)S(1)} async-done(((bf16[64,8,1536]{2,1,0:T(8,128)(2,1)}), bf16[64,8,1536]{2,1,0:T(8,128)(2,1)S(1)}, u32[]{:S(2)}, u32[]{:S(2)}) %all-to-all-start) | async-done | bytes 1572896 | tf_op jit(solution)/shard_map/all_to_all | solution.py:445
  58.6 1.2 shard_map.114
  59.8 0.1 collective-permute-start.3
  59.9 2.3 %shard_map.116 = bf16[512,1024]{1,0:T(8,128)(2,1)} custom-call(s32[2,128]{1,0:T(2,128)} %bitcast.17, bf16[128,4096]{1,0:T(8,128)(2,1)} %g_hbm.3), custom_call_target="tpu_custom_call" | custom-call | flops 100663296 | bytes 2098176 | tf_op jit(solution)/shard_map/pallas_call | solution.py:60
  62.3 10.9 %all-to-all-start.1 = ((bf16[64,8,1024]{2,1,0:T(8,128)(2,1)}), bf16[64,8,1024]{2,1,0:T(8,128)(2,1)}, u32[]{:S(2)}, u32[]{:S(2)}) async-start(bf16[64,8,1024]{2,1,0:T(8,128)(2,1)} %bitcast.14), calls=%async_computation.1 | async-start | bytes 2097152 | tf_op jit(solution)/shard_map/all_to_all | solution.py:445
  73.2 0.1 collective-permute-start.4
  73.3 9.7 %collective-permute-done.3.x1 = bf16[512,1024]{1,0:T(8,128)(2,1)S(1)} collective-permute-done((bf16[512,1024]{1,0:T(8,128)(2,1)}, bf16[512,1024]{1,0:T(8,128)(2,1)S(1)}, u32[]{:S(2)}, u32[]{:S(2)}) %collective-permute-start.3) | collective-permute-done | bytes 1048608 | tf_op jit(solution)/shard_map/ppermute | solution.py:441
  83.0 0.4 collective-permute-start.6
  83.4 0.6 copy-done.12
  84.0 1.0 copy-done.13
  84.9 0.8 collective-permute-done.5.x3
  85.8 5.9 %shard_map.115 = (f32[192,512]{1,0:T(8,128)}, f32[192,512]{1,0:T(8,128)}, bf16[192,512]{1,0:T(8,128)(2,1)}) custom-call(bf16[512,1024]{1,0:T(8,128)(2,1)} %get-tuple-element.59.x0, bf16[512,1024]{1,0:T(8,128)(2,1)} %copy-done.12, bf16[512,1024]{1,0:T(8,128)(2,1)} %copy-done.13, bf16[512,1024]{1,0:T(8,128)(2,1)} %collective-permute-done.5.x3, ...), custom_call_target="tpu_custom_call" | custom-call | flops 1610612736 | bytes 8323072 | tf_op jit(solution)/shard_map/pallas_call | solution.py:60
  91.7 10.0 %all-to-all-done.1 = bf16[64,8,1024]{2,1,0:T(8,128)(2,1)} async-done(((bf16[64,8,1024]{2,1,0:T(8,128)(2,1)}), bf16[64,8,1024]{2,1,0:T(8,128)(2,1)}, u32[]{:S(2)}, u32[]{:S(2)}) %all-to-all-start.1) | async-done | bytes 1048608 | tf_op jit(solution)/shard_map/all_to_all | solution.py:445
  101.7 3.6 %shard_map.117 = (f32[192,512]{1,0:T(8,128)}, f32[192,512]{1,0:T(8,128)}) custom-call(bf16[512,512]{1,0:T(8,128)(2,1)} %copy-done.1, bf16[512,512]{1,0:T(8,128)(2,1)} %collective-permute-done.6.g1, bf16[512,1024]{1,0:T(8,128)(2,1)} %bitcast.4.gd.gd0, bf16[1,192,4096]{2,1,0:T(8,128)(2,1)} %down_hbm.3, bf16[192,2048]{1,0:T(8,128)(2,1)} %collective-permute-done.1.near_hbm), custom_call_target="tpu_custom_call" | custom-call | flops 805306368 | bytes 5242880 | tf_op jit(solution)/shard_map/pallas_call | solution.py:60
  105.5 1.9 %collective-permute-done.7.got_hbm = f32[192,512]{1,0:T(8,128)S(1)} collective-permute-done((f32[192,512]{1,0:T(8,128)}, f32[192,512]{1,0:T(8,128)S(1)}, u32[]{:S(2)}, u32[]{:S(2)}) %collective-permute-start.7) | collective-permute-done | bytes 393248 | tf_op jit(solution)/shard_map/ppermute | solution.py:441
  107.4 1.0 copy-done.6
  108.4 1.4 shard_map.118.own_hbm.pack_hbm
  109.8 0.4 collective-permute-start.9
  110.2 2.0 %shard_map.120 = bf16[384,1024]{1,0:T(8,128)(2,1)} custom-call(bf16[384,2048]{1,0:T(8,128)(2,1)} %copy-done.10), custom_call_target="tpu_custom_call" | custom-call | flops 1000 | bytes 2359296 | tf_op jit(solution)/shard_map/pallas_call | solution.py:60
  112.3 0.5 collective-permute-start.11
  112.7 0.8 copy-done.11
  113.5 4.3 %shard_map.119.begun_hbm = f32[512,1024]{1,0:T(8,128)} custom-call(bf16[400,512]{1,0:T(8,128)(2,1)} %copy-done, bf16[400,512]{1,0:T(8,128)(2,1)} %copy-done.11, bf16[1,192,4096]{2,1,0:T(8,128)(2,1)} %gate_hbm.7, bf16[1,192,4096]{2,1,0:T(8,128)(2,1)} %up_hbm.7, bf16[384,1024]{1,0:T(8,128)(2,1)} %collective-permute-done.both_hbm), custom_call_target="tpu_custom_call" | custom-call | flops 805306368 | bytes 6848512 | tf_op jit(solution)/shard_map/pallas_call | solution.py:60
  117.8 4.2 %collective-permute-done.8.far_hbm = bf16[400,512]{1,0:T(8,128)(2,1)S(1)} collective-permute-done((bf16[400,512]{1,0:T(8,128)(2,1)S(1)}, bf16[400,512]{1,0:T(8,128)(2,1)S(1)}, u32[]{:S(2)}, u32[]{:S(2)}) %collective-permute-start.8) | collective-permute-done | bytes 409632 | tf_op jit(solution)/shard_map/ppermute | solution.py:441
  122.0 1.7 %collective-permute-done.10.last_hbm = bf16[400,512]{1,0:T(8,128)(2,1)S(1)} collective-permute-done((bf16[400,512]{1,0:T(8,128)(2,1)S(1)}, bf16[400,512]{1,0:T(8,128)(2,1)S(1)}, u32[]{:S(2)}, u32[]{:S(2)}) %collective-permute-start.10) | collective-permute-done | bytes 409632 | tf_op jit(solution)/shard_map/ppermute | solution.py:441
  123.7 0.8 copy-done.19
  124.5 4.5 %shard_map.121 = bf16[512,1152]{1,0:T(8,128)(2,1)} custom-call(f32[512,1024]{1,0:T(8,128)} %shard_map.119.begun_hbm, bf16[400,512]{1,0:T(8,128)(2,1)} %copy-done, bf16[400,512]{1,0:T(8,128)(2,1)} %copy-done.11, bf16[400,512]{1,0:T(8,128)(2,1)} %copy-done.18, bf16[400,512]{1,0:T(8,128)(2,1)} %copy-done.19, bf16[384,2048]{1,0:T(8,128)(2,1)} %copy-done.10, ...), custom_call_target="tpu_custom_call" | custom-call | flops 805306368 | bytes 7274496 | tf_op jit(solution)/shard_map/pallas_call | solution.py:60
  129.1 6.9 %all-to-all-start.2 = ((bf16[64,8,1152]{2,1,0:T(8,128)(2,1)}), bf16[64,8,1152]{2,1,0:T(8,128)(2,1)S(1)}, u32[]{:S(2)}, u32[]{:S(2)}) async-start(bf16[64,8,1152]{2,1,0:T(8,128)(2,1)} %bitcast.13), calls=%async_computation.2 | async-start | bytes 2359296 | tf_op jit(solution)/shard_map/all_to_all | solution.py:452
  136.0 0.1 collective-permute-start.14
  136.1 0.5 collective-permute-start.12
  136.6 0.1 collective-permute-start.13
  136.7 4.6 %shard_map.122 = (bf16[1,192,4096]{2,1,0:T(8,128)(2,1)}, bf16[1,192,4096]{2,1,0:T(8,128)(2,1)}) custom-call(bf16[400,512]{1,0:T(8,128)(2,1)} %copy-done, bf16[512,1024]{1,0:T(8,128)(2,1)} %get-tuple-element.59.x0, bf16[512,1024]{1,0:T(8,128)(2,1)} %copy-done.12, bf16[512,1024]{1,0:T(8,128)(2,1)} %copy-done.13, bf16[512,1024]{1,0:T(8,128)(2,1)} %collective-permute-done.5.x3), custom_call_target="tpu_custom_call" | custom-call | flops 1610612736 | bytes 7749632 | tf_op jit(solution)/shard_map/pallas_call | solution.py:60
  141.4 0.8 copy-done.16
  142.2 0.2 copy-done.17
  142.4 1.0 copy-done.14
  143.4 3.9 %shard_map.123 = bf16[1,192,4096]{2,1,0:T(8,128)(2,1)} custom-call(bf16[192,512]{1,0:T(8,128)(2,1)} %get-tuple-element.89.hidden_hbm, bf16[512,512]{1,0:T(8,128)(2,1)} %copy-done.1, bf16[512,512]{1,0:T(8,128)(2,1)} %collective-permute-done.6.g1, bf16[512,512]{1,0:T(8,128)(2,1)} %copy-done.16, bf16[512,512]{1,0:T(8,128)(2,1)} %copy-done.17, ...), custom_call_target="tpu_custom_call" | custom-call | flops 805306368 | bytes 5963776 | tf_op jit(solution)/shard_map/pallas_call | solution.py:60
  147.3 22.3 %all-to-all-done.2 = bf16[64,8,1152]{2,1,0:T(8,128)(2,1)S(1)} async-done(((bf16[64,8,1152]{2,1,0:T(8,128)(2,1)}), bf16[64,8,1152]{2,1,0:T(8,128)(2,1)S(1)}, u32[]{:S(2)}, u32[]{:S(2)}) %all-to-all-start.2) | async-done | bytes 1179680 | tf_op jit(solution)/shard_map/all_to_all | solution.py:452
  169.5 1.9 %shard_map.124 = (bf16[128,1024]{1,0:T(8,128)(2,1)}, f32[2,128]{1,0:T(2,128)}) custom-call(bf16[128,512]{1,0:T(8,128)(2,1)S(1)} %copy-done.7, bf16[128,512]{1,0:T(8,128)(2,1)S(1)} %copy-done.8, bf16[512,1152]{1,0:T(8,128)(2,1)S(1)} %bitcast.10, f32[2,128]{1,0:T(2,128)S(1)} %bitcast.11), custom_call_target="tpu_custom_call" | custom-call | flops 201326592 | bytes 1705984 | tf_op jit(solution)/shard_map/pallas_call | solution.py:60
  (43 shorter events, 0.2 us)
Async XLA Ops:
  3.2 55.4 %all-to-all-start = ((bf16[64,8,1536]{2,1,0:T(8,128)(2,1)}), bf16[64,8,1536]{2,1,0:T(8,128)(2,1)S(1)}, u32[]{:S(2)}, u32[]{:S(2)}) async-start(bf16[64,8,1536]{2,1,0:T(8,128)(2,1)} %bitcast.12), calls=%async_computation | async-start | bytes 3145728 | tf_op jit(solution)/shard_map/all_to_all | solution.py:445
  19.6 35.9 %collective-permute-start.2 = (bf16[384,2048]{1,0:T(8,128)(2,1)}, bf16[384,2048]{1,0:T(8,128)(2,1)S(1)}, u32[]{:S(2)}, u32[]{:S(2)}) collective-permute-start(bf16[384,2048]{1,0:T(8,128)(2,1)} %shard_map.113), channel_id=1, source_target_pairs={{0,128},{128,0},{1,129},{129,1},{2,130},{130,2},{3,131},{131,3},{4... | collective-permute-start | bytes 4718600 | tf_op jit(solution)/shard_map/ppermute | solution.py:441
  22.4 2.7 %collective-permute-start = (bf16[384,1024]{1,0:T(8,128)(2,1)}, bf16[384,1024]{1,0:T(8,128)(2,1)}, u32[]{:S(2)}, u32[]{:S(2)}) collective-permute-start(bf16[384,1024]{1,0:T(8,128)(2,1)} %get-tuple-element.54), channel_id=1, source_target_pairs={{0,64},{64,0},{1,65},{65,1},{2,66},{66,2},{3,67},{67,3},{4,68},{68... | collective-permute-start | bytes 2359304 | tf_op jit(solution)/shard_map/ppermute | solution.py:441
  22.6 3.7 %collective-permute-start.1 = (bf16[192,2048]{1,0:T(8,128)(2,1)}, bf16[192,2048]{1,0:T(8,128)(2,1)}, u32[]{:S(2)}, u32[]{:S(2)}) collective-permute-start(bf16[192,2048]{1,0:T(8,128)(2,1)} %get-tuple-element.55), channel_id=1, source_target_pairs={{0,64},{64,0},{1,65},{65,1},{2,66},{66,2},{3,67},{67,3},{4,68},{68... | collective-permute-start | bytes 2359304 | tf_op jit(solution)/shard_map/ppermute | solution.py:441
  55.4 3.2 %copy-start.10 = (bf16[384,2048]{1,0:T(8,128)(2,1)}, bf16[384,2048]{1,0:T(8,128)(2,1)S(1)}, u32[]{:S(2)}) copy-start(bf16[384,2048]{1,0:T(8,128)(2,1)S(1)} %collective-permute-done.2.both_hbm.far_both) | copy-start | bytes 4718596
  59.8 23.2 %copy-start.1 = (bf16[512,512]{1,0:T(8,128)(2,1)}, bf16[512,512]{1,0:T(8,128)(2,1)S(1)}, u32[]{:S(2)}) copy-start(bf16[512,512]{1,0:T(8,128)(2,1)S(1)} %get-tuple-element.90.g0) | copy-start | bytes 1572868
  59.8 23.1 %collective-permute-start.3 = (bf16[512,1024]{1,0:T(8,128)(2,1)}, bf16[512,1024]{1,0:T(8,128)(2,1)S(1)}, u32[]{:S(2)}, u32[]{:S(2)}) collective-permute-start(bf16[512,1024]{1,0:T(8,128)(2,1)} %get-tuple-element.59.x0), channel_id=1, source_target_pairs={{0,128},{128,0},{1,129},{129,1},{2,130},{130,2},{3,131},{131,3},{4... | collective-permute-start | bytes 3145736 | tf_op jit(solution)/shard_map/ppermute | solution.py:441
  62.3 39.4 %all-to-all-start.1 = ((bf16[64,8,1024]{2,1,0:T(8,128)(2,1)}), bf16[64,8,1024]{2,1,0:T(8,128)(2,1)}, u32[]{:S(2)}, u32[]{:S(2)}) async-start(bf16[64,8,1024]{2,1,0:T(8,128)(2,1)} %bitcast.14), calls=%async_computation.1 | async-start | bytes 2097152 | tf_op jit(solution)/shard_map/all_to_all | solution.py:445
  73.2 10.8 %collective-permute-start.4 = (bf16[512,1024]{1,0:T(8,128)(2,1)}, bf16[512,1024]{1,0:T(8,128)(2,1)S(1)}, u32[]{:S(2)}, u32[]{:S(2)}) collective-permute-start(bf16[512,1024]{1,0:T(8,128)(2,1)} %get-tuple-element.59.x0), channel_id=1, source_target_pairs={{0,64},{64,0},{1,65},{65,1},{2,66},{66,2},{3,67},{67,3},{4,68},{68... | collective-permute-start | bytes 3145736 | tf_op jit(solution)/shard_map/ppermute | solution.py:441
  83.0 1.0 copy-start.12
  83.0 2.8 %collective-permute-start.5 = (bf16[512,1024]{1,0:T(8,128)(2,1)S(1)}, bf16[512,1024]{1,0:T(8,128)(2,1)}, u32[]{:S(2)}, u32[]{:S(2)}) collective-permute-start(bf16[512,1024]{1,0:T(8,128)(2,1)S(1)} %collective-permute-done.3.x1), channel_id=1, source_target_pairs={{0,64},{64,0},{1,65},{65,1},{2,66},{66,2},{3,67},{67,3},{4,68},{68... | collective-permute-start | bytes 3145736 | tf_op jit(solution)/shard_map/ppermute | solution.py:441
  83.0 18.7 %collective-permute-start.6 = (bf16[512,512]{1,0:T(8,128)(2,1)S(1)}, bf16[512,512]{1,0:T(8,128)(2,1)}, u32[]{:S(2)}, u32[]{:S(2)}) collective-permute-start(bf16[512,512]{1,0:T(8,128)(2,1)S(1)} %get-tuple-element.90.g0), channel_id=1, source_target_pairs={{0,128},{128,0},{1,129},{129,1},{2,130},{130,2},{3,131},{131,3},{4... | collective-permute-start | bytes 1572872 | tf_op jit(solution)/shard_map/ppermute | solution.py:441
  84.0 1.0 copy-start.13
  101.7 5.7 %copy-start.3 = (bf16[192,512]{1,0:T(8,128)(2,1)S(1)}, bf16[192,512]{1,0:T(8,128)(2,1)}, u32[]{:S(2)}) copy-start(bf16[192,512]{1,0:T(8,128)(2,1)} %get-tuple-element.89.hidden_hbm) | copy-start | bytes 589828
  101.7 5.7 %copy-start.4 = (f32[192,512]{1,0:T(8,128)S(1)}, f32[192,512]{1,0:T(8,128)}, u32[]{:S(2)}) copy-start(f32[192,512]{1,0:T(8,128)} %get-tuple-element.73.act_hbm) | copy-start | bytes 1179652
  101.7 5.7 %copy-start.5 = (f32[192,512]{1,0:T(8,128)S(1)}, f32[192,512]{1,0:T(8,128)}, u32[]{:S(2)}) copy-start(f32[192,512]{1,0:T(8,128)} %get-tuple-element.74.pre_hbm) | copy-start | bytes 1179652
  105.4 2.0 %collective-permute-start.7 = (f32[192,512]{1,0:T(8,128)}, f32[192,512]{1,0:T(8,128)S(1)}, u32[]{:S(2)}, u32[]{:S(2)}) collective-permute-start(f32[192,512]{1,0:T(8,128)} %get-tuple-element.72), channel_id=1, source_target_pairs={{0,64},{64,0},{1,65},{65,1},{2,66},{66,2},{3,67},{67,3},{4,68},{68... | collective-permute-start | bytes 1179656 | tf_op jit(solution)/shard_map/ppermute | solution.py:441
  107.4 1.0 copy-start.6
  109.8 2.9 %copy-start = (bf16[400,512]{1,0:T(8,128)(2,1)}, bf16[400,512]{1,0:T(8,128)(2,1)S(1)}, u32[]{:S(2)}) copy-start(bf16[400,512]{1,0:T(8,128)(2,1)S(1)} %shard_map.118.own_hbm.pack_hbm) | copy-start | bytes 1228804
  109.8 2.9 %collective-permute-start.9 = (bf16[400,512]{1,0:T(8,128)(2,1)S(1)}, bf16[400,512]{1,0:T(8,128)(2,1)S(1)}, u32[]{:S(2)}, u32[]{:S(2)}) collective-permute-start(bf16[400,512]{1,0:T(8,128)(2,1)S(1)} %shard_map.118.own_hbm.pack_hbm), channel_id=1, source_target_pairs={{0,64},{64,0},{1,65},{65,1},{2,66},{66,2},{3,67},{67,3},{4,68},{68... | collective-permute-start | bytes 1228808 | tf_op jit(solution)/shard_map/ppermute | solution.py:441
  110.2 11.7 %collective-permute-start.8 = (bf16[400,512]{1,0:T(8,128)(2,1)S(1)}, bf16[400,512]{1,0:T(8,128)(2,1)S(1)}, u32[]{:S(2)}, u32[]{:S(2)}) collective-permute-start(bf16[400,512]{1,0:T(8,128)(2,1)S(1)} %shard_map.118.own_hbm.pack_hbm), channel_id=1, source_target_pairs={{0,128},{128,0},{1,129},{129,1},{2,130},{130,2},{3,131},{131,3},{4... | collective-permute-start | bytes 1228808 | tf_op jit(solution)/shard_map/ppermute | solution.py:441
  112.3 9.7 %collective-permute-start.11 = (bf16[384,1024]{1,0:T(8,128)(2,1)}, bf16[384,1024]{1,0:T(8,128)(2,1)S(1)}, u32[]{:S(2)}, u32[]{:S(2)}) collective-permute-start(bf16[384,1024]{1,0:T(8,128)(2,1)} %shard_map.120), channel_id=1, source_target_pairs={{0,64},{64,0},{1,65},{65,1},{2,66},{66,2},{3,67},{67,3},{4,68},{68... | collective-permute-start | bytes 2359304 | tf_op jit(solution)/shard_map/ppermute | solution.py:441
  112.7 0.8 copy-start.11
  122.0 1.8 %copy-start.18 = (bf16[400,512]{1,0:T(8,128)(2,1)}, bf16[400,512]{1,0:T(8,128)(2,1)S(1)}, u32[]{:S(2)}) copy-start(bf16[400,512]{1,0:T(8,128)(2,1)S(1)} %collective-permute-done.8.far_hbm) | copy-start | bytes 1228804
  122.0 1.7 %collective-permute-start.10 = (bf16[400,512]{1,0:T(8,128)(2,1)S(1)}, bf16[400,512]{1,0:T(8,128)(2,1)S(1)}, u32[]{:S(2)}, u32[]{:S(2)}) collective-permute-start(bf16[400,512]{1,0:T(8,128)(2,1)S(1)} %collective-permute-done.8.far_hbm), channel_id=1, source_target_pairs={{0,64},{64,0},{1,65},{65,1},{2,66},{66,2},{3,67},{67,3},{4,68},{68... | collective-permute-start | bytes 1228808 | tf_op jit(solution)/shard_map/ppermute | solution.py:441
  122.0 1.7 %copy-start.15 = (bf16[384,1024]{1,0:T(8,128)(2,1)}, bf16[384,1024]{1,0:T(8,128)(2,1)S(1)}, u32[]{:S(2)}) copy-start(bf16[384,1024]{1,0:T(8,128)(2,1)S(1)} %collective-permute-done.11.last_both) | copy-start | bytes 2359300
  123.7 0.8 copy-start.19
  129.0 7.0 %copy-start.2 = (bf16[512,512]{1,0:T(8,128)(2,1)S(1)}, bf16[512,512]{1,0:T(8,128)(2,1)}, u32[]{:S(2)}) copy-start(bf16[512,512]{1,0:T(8,128)(2,1)} %copy-done.1) | copy-start | bytes 1572868
  129.1 40.5 %all-to-all-start.2 = ((bf16[64,8,1152]{2,1,0:T(8,128)(2,1)}), bf16[64,8,1152]{2,1,0:T(8,128)(2,1)S(1)}, u32[]{:S(2)}, u32[]{:S(2)}) async-start(bf16[64,8,1152]{2,1,0:T(8,128)(2,1)} %bitcast.13), calls=%async_computation.2 | async-start | bytes 2359296 | tf_op jit(solution)/shard_map/all_to_all | solution.py:452
  136.0 5.4 %collective-permute-start.14 = (bf16[512,1024]{1,0:T(8,128)(2,1)}, bf16[512,1024]{1,0:T(8,128)(2,1)S(1)}, u32[]{:S(2)}, u32[]{:S(2)}) collective-permute-start(bf16[512,1024]{1,0:T(8,128)(2,1)} %bitcast.4.gd.gd0), channel_id=1, source_target_pairs={{0,64},{64,0},{1,65},{65,1},{2,66},{66,2},{3,67},{67,3},{4,68},{68... | collective-permute-start | bytes 3145736 | tf_op jit(solution)/shard_map/ppermute | solution.py:441
  136.1 5.3 %collective-permute-start.12 = (bf16[512,512]{1,0:T(8,128)(2,1)S(1)}, bf16[512,512]{1,0:T(8,128)(2,1)S(1)}, u32[]{:S(2)}, u32[]{:S(2)}) collective-permute-start(bf16[512,512]{1,0:T(8,128)(2,1)S(1)} %copy-done.2), channel_id=1, source_target_pairs={{0,64},{64,0},{1,65},{65,1},{2,66},{66,2},{3,67},{67,3},{4,68},{68... | collective-permute-start | bytes 1572872 | tf_op jit(solution)/shard_map/ppermute | solution.py:441
  136.6 4.8 %collective-permute-start.13 = (bf16[512,512]{1,0:T(8,128)(2,1)}, bf16[512,512]{1,0:T(8,128)(2,1)S(1)}, u32[]{:S(2)}, u32[]{:S(2)}) collective-permute-start(bf16[512,512]{1,0:T(8,128)(2,1)} %collective-permute-done.6.g1), channel_id=1, source_target_pairs={{0,64},{64,0},{1,65},{65,1},{2,66},{66,2},{3,67},{67,3},{4,68},{68... | collective-permute-start | bytes 1572872 | tf_op jit(solution)/shard_map/ppermute | solution.py:441
  141.3 28.2 %copy-start.7 = (bf16[128,512]{1,0:T(8,128)(2,1)S(1)}, bf16[128,512]{1,0:T(8,128)(2,1)}, u32[]{:S(2)}) copy-start(bf16[128,512]{1,0:T(8,128)(2,1)} %get-tuple-element.56.first_hbm) | copy-start | bytes 393220
  141.4 28.2 %copy-start.8 = (bf16[128,512]{1,0:T(8,128)(2,1)S(1)}, bf16[128,512]{1,0:T(8,128)(2,1)}, u32[]{:S(2)}) copy-start(bf16[128,512]{1,0:T(8,128)(2,1)} %get-tuple-element.57.second_hbm) | copy-start | bytes 393220
  141.4 28.2 %copy-start.9 = (f32[128,2]{0,1:T(2,128)S(1)}, f32[128,2]{0,1:T(2,128)}, u32[]{:S(2)}) copy-start(f32[128,2]{0,1:T(2,128)} %param.10) | copy-start | bytes 3076
  141.4 0.8 copy-start.16
  141.4 1.0 copy-start.17
  142.4 1.0 copy-start.14
